TPU v7x, 32 devices: a whole 2x2x4 slice. The times are simulated.
32 devices in a mesh: gy: 8 (over y, x, core), pa: 4 (over z).
Axes of the slice: x: 2, y: 2, z: 4, core: 2. Of those that a mesh axis runs over, the one named last changes fastest.
Arguments:
- spectral_velocity: float32 [3, 16, 512, 1536], P(None, 'gy', 'pa'), may hold values from -0.01913664 to 0.01913664
- inverse_spacing: float32 [16], P('gy'), may hold values from 0.25 to 1
Outputs:
- increment: float32 [3, 16, 1152, 1536], P(None, 'gy', 'pa')
- vorticity_peak: float32 [], replicated
All inputs are finite; a program needn't handle non-finite values.
Results may differ from a plain program's by a relative error of at most 0.00011.
Values sent between devices are 32-bit elements; how exact they have to be, the bound alone decides.
A program may use at most 128 MiB of HBM per device.

v0:
```python
import math

import numpy as np

import jax
import jax.numpy as jnp
from jax import lax
from jax.sharding import PartitionSpec as P

NX = 1536
NZ = 1152
KX = 512


def z_table(length, modes, parts):
    column = np.arange(modes)
    wave = np.where(column < modes // 2, column, column - modes)
    angles = (wave[None, :] * np.arange(length)[:, None] % length) * (2.0 * math.pi / length)
    cos, sin = np.cos(angles), np.sin(angles)
    scale = (wave * (2.0 * math.pi / length))[None, :]

    def lay(rr, ri, ir, ii):
        real = np.concatenate((rr, ri), 1).reshape(parts, 1, length // parts, 2 * modes)
        imag = np.concatenate((ir, ii), 1).reshape(parts, 1, length // parts, 2 * modes)
        both = np.concatenate((real, imag), 1)
        return both.reshape(parts, -1, 2 * modes).astype(np.float32)

    plain = lay(cos, -sin, sin, cos)
    slope = lay(-scale * sin, -scale * cos, scale * cos, -scale * sin)
    return plain, slope


def x_table(length, modes, parts):
    column = np.arange(modes)
    angles = (column[:, None] * np.arange(length)[None, :] % length) * (2.0 * math.pi / length)
    weight = np.where(column == 0, 1.0, 2.0)[:, None]
    both = np.stack((weight * np.cos(angles), -weight * np.sin(angles)))
    both = both.reshape(2, parts, modes // parts, length)
    return np.moveaxis(both, 1, 0).astype(np.float32)


def everywhere_max(value, axes):
    for axis in axes:
        count = lax.axis_size(axis)
        shift = 1
        while shift < count:
            pairs = [(i, (i + shift) % count) for i in range(count)]
            value = jnp.maximum(value, lax.ppermute(value, axis, pairs))
            shift *= 2
    return value


def body(spectral_velocity, inverse_spacing):
    planes, kx_local, width = spectral_velocity.shape[1:]
    parts = lax.axis_size("pa")
    levels = lax.axis_size("gy")
    me = lax.axis_index("pa")
    slab = NZ // parts
    plain, slope = z_table(NZ, width // 2, parts)
    order = (me - jnp.arange(parts)) % parts
    pieces = x_table(NX, KX, parts)
    pieces = np.concatenate([pieces[[-k % parts]] for k in range(2 * parts)])
    pieces = np.ascontiguousarray(np.moveaxis(pieces, 1, 0)).reshape(2, -1, NX)
    table_x = lax.dynamic_slice_in_dim(
        jnp.asarray(pieces), (parts - me) * kx_local, KX, axis=1
    ).reshape(2 * KX, NX)
    kx = (order[:, None] * kx_local + jnp.arange(kx_local)[None, :]).reshape(-1)
    wave_x = kx.astype(jnp.float32) * (2.0 * math.pi / NX)

    def exchange(modes, table):
        out = jnp.einsum(
            "dnk,fjmk->dfjnm", table, modes, precision=lax.Precision.HIGH,
            preferred_element_type=jnp.float32,
        )
        got = [lax.dynamic_index_in_dim(out, me, 0, keepdims=False)]
        for shift in range(1, parts):
            block = lax.dynamic_index_in_dim(out, (me + shift) % parts, 0, keepdims=False)
            got.append(lax.ppermute(block, "pa", [(i, (i + shift) % parts) for i in range(parts)]))
        whole = jnp.concatenate(got, axis=-1)
        return whole.reshape(whole.shape[:2] + (2, slab, KX))

    def to_x(hat):
        flat = jnp.concatenate((hat[..., 0, :, :], hat[..., 1, :, :]), axis=-1)
        return jnp.einsum(
            "...zm,mx->...zx", flat, table_x, precision=lax.Precision.HIGH,
            preferred_element_type=jnp.float32,
        )

    def turned(hat):
        return jnp.stack((-wave_x * hat[..., 1, :, :], wave_x * hat[..., 0, :, :]), axis=-3)

    u_modes, v_modes, w_modes = (spectral_velocity[c : c + 1] for c in range(3))
    uw_hat = exchange(jnp.concatenate((u_modes, w_modes)), plain)
    dzu_hat = exchange(u_modes, slope)[0]
    v_hat = exchange(v_modes, plain)[0]
    dzv_hat = exchange(v_modes, slope)[0]

    below = lax.ppermute(uw_hat[:, -1:], "gy", [(i, i + 1) for i in range(levels - 1)])
    above = lax.ppermute(uw_hat[:, :1], "gy", [(i + 1, i) for i in range(levels - 1)])
    spacing = inverse_spacing[None, :, None, None, None]
    lower = jnp.concatenate((below, uw_hat[:, :-1]), axis=1)
    upper = jnp.concatenate((uw_hat[:, 1:], above), axis=1)
    slope_y = (upper - lower) * spacing

    u, w = to_x(uw_hat[0]), to_x(uw_hat[1])
    vort_y = to_x(dzu_hat - turned(uw_hat[1]))
    v = to_x(v_hat)
    vort_z = to_x(turned(v_hat) - slope_y[0])
    vort_x = to_x(slope_y[1] - dzv_hat)
    lamb = jnp.stack(
        (v * vort_z - w * vort_y, w * vort_x - u * vort_z, u * vort_y - v * vort_x)
    )
    local_peak = jnp.max(vort_x * vort_x + vort_y * vort_y + vort_z * vort_z)
    magnitude = jnp.sqrt(everywhere_max(local_peak, ("gy", "pa")))
    return (lamb / (magnitude + 1e-06), magnitude)


def solution(mesh):
    placed = (P(None, "gy", "pa", None), P("gy"))
    return jax.shard_map(
        body,
        mesh=mesh,
        in_specs=placed,
        out_specs=(P(None, "gy", "pa", None), P()),
        check_vma=False,
    )
```

profile of v0, /device:TPU:0, one launch (start us, length us, event | category | flops | bytes accessed | tf_op | source)
XLA Modules:
  0.0 357.9 jit_solution(10813896155509421837)
XLA Ops:
  0.7 9.3 %fusion.33 = f32[4,576,2,128]{3,1,2,0:T(8,128)S(1)} fusion(f32[4,576,1536,1]{2,1,3,0:T(8,128)} %constant.115, f32[3,2,128,1536]{3,2,1,0:T(8,128)} %param.7), kind=kOutput, calls=%fused_computation.51 | convolution fusion | flops 5435817984 | bytes 18087936 | tf_op jit(solution)/shard_map/dnk,fjmk->dfjnm/dot_general | solution.py:71
  11.5 4.0 %collective-permute-start.1 = (f32[1,2,576,128]{3,2,1,0:T(8,128)}, f32[1,2,576,128]{3,2,1,0:T(8,128)}, u32[]{:S(2)}, u32[]{:S(2)}) collective-permute-start(f32[1,2,576,128]{3,2,1,0:T(8,128)} %get-tuple-element.43), channel_id=1, source_target_pairs={{0,2},{1,3},{2,0},{3,1},{4,6},{5,7},{6,4},{7,5},{8,10},{9,11},{10,... | collective-permute-start | bytes 1769480 | tf_op jit(solution)/shard_map/ppermute | solution.py:78
  17.3 14.3 %fusion.1 = f32[2,2,128,4,576]{2,4,3,1,0:T(8,128)S(1)} fusion(f32[4,576,1536,1,1]{2,1,0,4,3:T(8,128)} %constant.116, f32[1,2,128,1536]{3,2,1,0:T(8,128)S(1)} %get-tuple-element.17, f32[1,2,128,1536]{3,2,1,0:T(8,128)S(1)} %get-tuple-element.16), kind=kOutput, calls=%fused_computation.10 | convolution fusion | flops 10872422400 | bytes 22020096 | tf_op jit(solution)/shard_map/dnk,fjmk->dfjnm/dot_general | solution.py:71
  33.6 4.0 %collective-permute-start.5 = (f32[2,2,576,128]{3,2,1,0:T(8,128)}, f32[2,2,576,128]{3,2,1,0:T(8,128)}, u32[]{:S(2)}, u32[]{:S(2)}) collective-permute-start(f32[2,2,576,128]{3,2,1,0:T(8,128)} %get-tuple-element.14), channel_id=1, source_target_pairs={{0,3},{1,0},{2,1},{3,2},{4,7},{5,4},{6,5},{7,6},{8,11},{9,8},{10,9... | collective-permute-start | bytes 3538952 | tf_op jit(solution)/shard_map/ppermute | solution.py:78
  37.7 6.3 %fusion.32 = f32[4,576,2,128]{3,1,2,0:T(8,128)S(1)} fusion(f32[4,576,1536,1]{2,1,3,0:T(8,128)S(1)} %bitcast.236, f32[3,2,128,1536]{3,2,1,0:T(8,128)S(1)} %copy-done), kind=kOutput, calls=%fused_computation.50 | convolution fusion | flops 5435817984 | bytes 18087936 | tf_op jit(solution)/shard_map/dnk,fjmk->dfjnm/dot_general | solution.py:71
  44.0 6.4 %fusion.30 = f32[4,576,2,128]{3,1,2,0:T(8,128)S(1)} fusion(f32[4,576,1536,1]{2,1,3,0:T(8,128)S(1)} %bitcast.236, f32[3,2,128,1536]{3,2,1,0:T(8,128)S(1)} %copy-done), kind=kOutput, calls=%fused_computation.48 | convolution fusion | flops 5435817984 | bytes 18087936 | tf_op jit(solution)/shard_map/dnk,fjmk->dfjnm/dot_general | solution.py:71
  52.1 28.5 %collective-permute-done.1 = f32[1,2,576,128]{3,2,1,0:T(8,128)} collective-permute-done((f32[1,2,576,128]{3,2,1,0:T(8,128)}, f32[1,2,576,128]{3,2,1,0:T(8,128)}, u32[]{:S(2)}, u32[]{:S(2)}) %collective-permute-start.1) | collective-permute-done | bytes 589856 | tf_op jit(solution)/shard_map/ppermute | solution.py:78
  81.9 3.3 constant_dynamic-slice_fusion.3
  85.3 45.5 %collective-permute-done.2 = f32[1,2,576,128]{3,2,1,0:T(8,128)S(1)} collective-permute-done((f32[1,2,576,128]{3,2,1,0:T(8,128)}, f32[1,2,576,128]{3,2,1,0:T(8,128)S(1)}, u32[]{:S(2)}, u32[]{:S(2)}) %collective-permute-start.2) | collective-permute-done | bytes 589856 | tf_op jit(solution)/shard_map/ppermute | solution.py:78
  130.8 64.0 %collective-permute-start.11 = (f32[1,2,576,128]{3,2,1,0:T(8,128)}, f32[1,2,576,128]{3,2,1,0:T(8,128)}, u32[]{:S(2)}, u32[]{:S(2)}) collective-permute-start(f32[1,2,576,128]{3,2,1,0:T(8,128)} %get-tuple-element.38), channel_id=1, source_target_pairs={{0,1},{1,2},{2,3},{3,0},{4,5},{5,6},{6,7},{7,4},{8,9},{9,10},{10,1... | collective-permute-start | bytes 1769480 | tf_op jit(solution)/shard_map/ppermute | solution.py:78
  206.0 5.9 %fusion.26 = f32[2,288,1536]{2,1,0:T(8,128)S(1)} fusion(f32[1024,1536,1]{1,0,2:T(8,128)S(1)} %bitcast.229, f32[2,288,512]{2,1,0:T(8,128)S(1)} %get-tuple-element.33, f32[2,288,512]{2,1,0:T(8,128)S(1)} %get-tuple-element.32), kind=kOutput, calls=%fused_computation.43 | convolution fusion | flops 5436407808 | bytes 12189696 | tf_op jit(solution)/shard_map/...zm,mx->...zx/dot_general | solution.py:84
  212.1 7.8 %fusion.14 = f32[2,288,1536]{2,1,0:T(8,128)} fusion(f32[1024,1536,1]{1,0,2:T(8,128)S(1)} %bitcast.230, f32[2,288,512]{2,1,0:T(8,128)S(1)} %get-tuple-element.19, f32[2,288,512]{2,1,0:T(8,128)S(1)} %get-tuple-element.18), kind=kOutput, calls=%fused_computation.28 | convolution fusion | flops 5436407808 | bytes 12189696 | tf_op jit(solution)/shard_map/...zm,mx->...zx/dot_general | solution.py:84
  226.3 3.7 %fusion = f32[2,2,2,288,512]{4,3,1,2,0:T(8,128)S(1)} fusion(f32[2,1,2,288,512]{4,3,1,2,0:T(8,128)} %collective-permute-done.6, f32[2,1,2,288,512]{4,3,1,2,0:T(8,128)S(1)} %get-tuple-element.10, f32[2,1,2,288,512]{4,3,1,2,0:T(8,128)S(1)} %get-tuple-element.11, f32[2,1,2,288,512]{4,3,1,2,0:T(8,128)} %copy-done.2, f32[2]{0:T(128)S(1)} %copy-done.5), kind=kLoop, calls=%fused_computation.3 | loop fusion | flops 4718592 | bytes 14155784 | tf_op jit(solution)/shard_map/mul | solution.py:103
  230.1 30.9 %collective-permute-done.9 = f32[1,2,576,128]{3,2,1,0:T(8,128)} collective-permute-done((f32[1,2,576,128]{3,2,1,0:T(8,128)}, f32[1,2,576,128]{3,2,1,0:T(8,128)}, u32[]{:S(2)}, u32[]{:S(2)}) %collective-permute-start.9) | collective-permute-done | bytes 589856 | tf_op jit(solution)/shard_map/ppermute | solution.py:78
  264.6 7.7 %fusion.22 = f32[2,288,1536]{2,1,0:T(8,128)} fusion(f32[1024,1536,1]{1,0,2:T(8,128)S(1)} %bitcast.231, f32[2,288,512]{2,1,0:T(8,128)S(1)} %get-tuple-element.35, f32[2,288,512]{2,1,0:T(8,128)S(1)} %get-tuple-element.34), kind=kOutput, calls=%fused_computation.39 | convolution fusion | flops 5436407808 | bytes 12189696 | tf_op jit(solution)/shard_map/...zm,mx->...zx/dot_general | solution.py:84
  272.3 8.0 %fusion.18 = f32[2,288,1536]{2,1,0:T(8,128)} fusion(f32[1024,1536,1]{1,0,2:T(8,128)S(1)} %bitcast.232, f32[2,288,512]{2,1,0:T(8,128)S(1)} %get-tuple-element.25, f32[2,288,512]{2,1,0:T(8,128)S(1)} %get-tuple-element.24), kind=kOutput, calls=%fused_computation.34 | convolution fusion | flops 5436407808 | bytes 12189696 | tf_op jit(solution)/shard_map/...zm,mx->...zx/dot_general | solution.py:84
  280.3 7.7 %fusion.10 = f32[2,288,1536]{2,1,0:T(8,128)} fusion(f32[1024,1536,1]{1,0,2:T(8,128)S(1)} %bitcast.233, f32[2,288,512]{2,1,0:T(8,128)S(1)} %get-tuple-element.21, f32[2,288,512]{2,1,0:T(8,128)S(1)} %get-tuple-element.20), kind=kOutput, calls=%fused_computation.24 | convolution fusion | flops 5436407808 | bytes 12189696 | tf_op jit(solution)/shard_map/...zm,mx->...zx/dot_general | solution.py:84
  287.9 13.6 %add_reduce_fusion = (f32[]{:T(128)}, f32[1,2,288,1536]{3,2,1,0:T(8,128)}, f32[1,2,288,1536]{3,2,1,0:T(8,128)}, f32[1,2,288,1536]{3,2,1,0:T(8,128)}) fusion(f32[2,288,1536]{2,1,0:T(8,128)} %fusion.10, f32[2,288,1536]{2,1,0:T(8,128)} %fusion.18, f32[2,288,1536]{2,1,0:T(8,128)} %fusion.22, f32[2,288,1536]{2,1,0:T(8,128)S(1)} %fusion.26, ...), kind=kOutput, calls=%fused_computation.5 | convolution fusion | flops 5449678848 | bytes 36962308 | tf_op jit(solution)/shard_map/...zm,mx->...zx/dot_general | solution.py:84
  301.5 7.7 %collective-permute-start.14 = (f32[]{:T(128)}, f32[]{:T(128)}, u32[]{:S(2)}, u32[]{:S(2)}) collective-permute-start(f32[]{:T(128)} %get-tuple-element.2), channel_id=1, source_target_pairs={{0,4},{4,8},{8,12},{12,16},{16,20},{20,24},{24,28},{28,0},{1,5},{5... | collective-permute-start | bytes 20 | tf_op jit(solution)/shard_map/ppermute | solution.py:48
  311.4 13.4 %collective-permute-start.15 = (f32[]{:T(128)}, f32[]{:T(128)}, u32[]{:S(2)}, u32[]{:S(2)}) collective-permute-start(f32[]{:T(128)} %max.15), channel_id=1, source_target_pairs={{0,8},{4,12},{8,16},{12,20},{16,24},{20,28},{24,0},{28,4},{1,9},{5... | collective-permute-start | bytes 20 | tf_op jit(solution)/shard_map/ppermute | solution.py:48
  324.9 3.7 %collective-permute-done.15 = f32[]{:T(128)} collective-permute-done((f32[]{:T(128)}, f32[]{:T(128)}, u32[]{:S(2)}, u32[]{:S(2)}) %collective-permute-start.15) | collective-permute-done | bytes 36 | tf_op jit(solution)/shard_map/ppermute | solution.py:48
  329.2 5.9 %collective-permute-start.16 = (f32[]{:T(128)}, f32[]{:T(128)}, u32[]{:S(2)}, u32[]{:S(2)}) collective-permute-start(f32[]{:T(128)} %max.16), channel_id=1, source_target_pairs={{0,16},{4,20},{8,24},{12,28},{16,0},{20,4},{24,8},{28,12},{1,17},{... | collective-permute-start | bytes 20 | tf_op jit(solution)/shard_map/ppermute | solution.py:48
  337.9 3.4 collective-permute-done.17
  347.2 9.4 %maximum_divide_fusion = f32[3,2,288,1536]{3,2,1,0:T(8,128)} fusion(f32[1,2,288,1536]{3,2,1,0:T(8,128)} %get-tuple-element.3, f32[1,2,288,1536]{3,2,1,0:T(8,128)} %get-tuple-element.4, f32[1,2,288,1536]{3,2,1,0:T(8,128)} %get-tuple-element.5, f32[]{:T(128)S(6)} %add.124), kind=kLoop, calls=%fused_computation | loop fusion | flops 7962624 | bytes 21233668 | tf_op jit(solution)/shard_map/div | solution.py:115
  (69 shorter events, 37.1 us)
Async XLA Ops:
  11.5 69.1 %collective-permute-start.1 = (f32[1,2,576,128]{3,2,1,0:T(8,128)}, f32[1,2,576,128]{3,2,1,0:T(8,128)}, u32[]{:S(2)}, u32[]{:S(2)}) collective-permute-start(f32[1,2,576,128]{3,2,1,0:T(8,128)} %get-tuple-element.43), channel_id=1, source_target_pairs={{0,2},{1,3},{2,0},{3,1},{4,6},{5,7},{6,4},{7,5},{8,10},{9,11},{10,... | collective-permute-start | bytes 1769480 | tf_op jit(solution)/shard_map/ppermute | solution.py:78
  15.5 69.7 %collective-permute-start = (f32[1,2,576,128]{3,2,1,0:T(8,128)}, f32[1,2,576,128]{3,2,1,0:T(8,128)}, u32[]{:S(2)}, u32[]{:S(2)}) collective-permute-start(f32[1,2,576,128]{3,2,1,0:T(8,128)} %get-tuple-element.44), channel_id=1, source_target_pairs={{0,1},{1,2},{2,3},{3,0},{4,5},{5,6},{6,7},{7,4},{8,9},{9,10},{10,1... | collective-permute-start | bytes 1769480 | tf_op jit(solution)/shard_map/ppermute | solution.py:78
  17.3 20.3 %slice-start = ((s8[14155776]{0:T(1024)(128)(4,1)}), s8[4194304]{0:T(1024)(128)(4,1)S(1)}, s32[]{:S(2)}) async-start(s8[14155776]{0:T(1024)(128)(4,1)} %bitcast.235), calls=%async_computation | async-start | bytes 8388608
  17.3 20.3 %slice-start.1 = ((s8[14155776]{0:T(1024)(128)(4,1)}), s8[4194304]{0:T(1024)(128)(4,1)S(1)}, s32[]{:S(2)}) async-start(s8[14155776]{0:T(1024)(128)(4,1)} %bitcast.235), calls=%async_computation.1 | async-start | bytes 8388608
  17.3 20.3 %slice-start.2 = ((s8[14155776]{0:T(1024)(128)(4,1)}), s8[1572864]{0:T(1024)(128)(4,1)S(1)}, s32[]{:S(2)}) async-start(s8[14155776]{0:T(1024)(128)(4,1)} %bitcast.235), calls=%async_computation.2 | async-start | bytes 3145728
  33.6 162.8 %collective-permute-start.3 = (f32[2,2,576,128]{3,2,1,0:T(8,128)}, f32[2,2,576,128]{3,2,1,0:T(8,128)}, u32[]{:S(2)}, u32[]{:S(2)}) collective-permute-start(f32[2,2,576,128]{3,2,1,0:T(8,128)} %get-tuple-element.13), channel_id=1, source_target_pairs={{0,1},{1,2},{2,3},{3,0},{4,5},{5,6},{6,7},{7,4},{8,9},{9,10},{10,1... | collective-permute-start | bytes 3538952 | tf_op jit(solution)/shard_map/ppermute | solution.py:78
  33.6 163.7 %collective-permute-start.5 = (f32[2,2,576,128]{3,2,1,0:T(8,128)}, f32[2,2,576,128]{3,2,1,0:T(8,128)}, u32[]{:S(2)}, u32[]{:S(2)}) collective-permute-start(f32[2,2,576,128]{3,2,1,0:T(8,128)} %get-tuple-element.14), channel_id=1, source_target_pairs={{0,3},{1,0},{2,1},{3,2},{4,7},{5,4},{6,5},{7,6},{8,11},{9,8},{10,9... | collective-permute-start | bytes 3538952 | tf_op jit(solution)/shard_map/ppermute | solution.py:78
  37.6 159.7 %collective-permute-start.4 = (f32[2,2,576,128]{3,2,1,0:T(8,128)}, f32[2,2,576,128]{3,2,1,0:T(8,128)}, u32[]{:S(2)}, u32[]{:S(2)}) collective-permute-start(f32[2,2,576,128]{3,2,1,0:T(8,128)} %get-tuple-element.15), channel_id=1, source_target_pairs={{0,2},{1,3},{2,0},{3,1},{4,6},{5,7},{6,4},{7,5},{8,10},{9,11},{10,... | collective-permute-start | bytes 3538952 | tf_op jit(solution)/shard_map/ppermute | solution.py:78
  80.6 50.2 %collective-permute-start.2 = (f32[1,2,576,128]{3,2,1,0:T(8,128)}, f32[1,2,576,128]{3,2,1,0:T(8,128)S(1)}, u32[]{:S(2)}, u32[]{:S(2)}) collective-permute-start(f32[1,2,576,128]{3,2,1,0:T(8,128)} %get-tuple-element.45), channel_id=1, source_target_pairs={{0,3},{1,0},{2,1},{3,2},{4,7},{5,4},{6,5},{7,6},{8,11},{9,8},{10,9... | collective-permute-start | bytes 1769480 | tf_op jit(solution)/shard_map/ppermute | solution.py:78
  81.9 112.9 %copy-start.1 = (f32[1,576,2,128]{3,1,2,0:T(8,128)S(1)}, f32[1,576,2,128]{3,1,2,0:T(8,128)}, u32[]{:S(2)}) copy-start(f32[1,576,2,128]{3,1,2,0:T(8,128)} %get-tuple-element.42) | copy-start | bytes 1769476
  85.2 134.7 %collective-permute-start.12 = (f32[1,2,576,128]{3,2,1,0:T(8,128)}, f32[1,2,576,128]{3,2,1,0:T(8,128)}, u32[]{:S(2)}, u32[]{:S(2)}) collective-permute-start(f32[1,2,576,128]{3,2,1,0:T(8,128)} %get-tuple-element.37), channel_id=1, source_target_pairs={{0,2},{1,3},{2,0},{3,1},{4,6},{5,7},{6,4},{7,5},{8,10},{9,11},{10,... | collective-permute-start | bytes 1769480 | tf_op jit(solution)/shard_map/ppermute | solution.py:78
  130.8 99.3 %collective-permute-start.11 = (f32[1,2,576,128]{3,2,1,0:T(8,128)}, f32[1,2,576,128]{3,2,1,0:T(8,128)}, u32[]{:S(2)}, u32[]{:S(2)}) collective-permute-start(f32[1,2,576,128]{3,2,1,0:T(8,128)} %get-tuple-element.38), channel_id=1, source_target_pairs={{0,1},{1,2},{2,3},{3,0},{4,5},{5,6},{6,7},{7,4},{8,9},{9,10},{10,1... | collective-permute-start | bytes 1769480 | tf_op jit(solution)/shard_map/ppermute | solution.py:78
  197.3 32.8 %collective-permute-start.13 = (f32[1,2,576,128]{3,2,1,0:T(8,128)S(1)}, f32[1,2,576,128]{3,2,1,0:T(8,128)}, u32[]{:S(2)}, u32[]{:S(2)}) collective-permute-start(f32[1,2,576,128]{3,2,1,0:T(8,128)S(1)} %copy-done.4), channel_id=1, source_target_pairs={{0,3},{1,0},{2,1},{3,2},{4,7},{5,4},{6,5},{7,6},{8,11},{9,8},{10,9... | collective-permute-start | bytes 1769480 | tf_op jit(solution)/shard_map/ppermute | solution.py:78
  200.2 21.1 %collective-permute-start.7 = (f32[2,1,2,288,512]{4,3,1,2,0:T(8,128)S(1)}, f32[2,1,2,288,512]{4,3,1,2,0:T(8,128)S(1)}, u32[]{:S(2)}, u32[]{:S(2)}) collective-permute-start(f32[2,1,2,288,512]{4,3,1,2,0:T(8,128)S(1)} %get-tuple-element.10), channel_id=1, source_target_pairs={{0,4},{4,8},{8,12},{12,16},{16,20},{20,24},{24,28},{1,5},{5,9},{9,... | collective-permute-start | bytes 7077896 | tf_op jit(solution)/shard_map/ppermute | solution.py:98
  201.6 20.3 %collective-permute-start.6 = (f32[2,1,2,288,512]{4,3,1,2,0:T(8,128)S(1)}, f32[2,1,2,288,512]{4,3,1,2,0:T(8,128)}, u32[]{:S(2)}, u32[]{:S(2)}) collective-permute-start(f32[2,1,2,288,512]{4,3,1,2,0:T(8,128)S(1)} %get-tuple-element.11), channel_id=1, source_target_pairs={{4,0},{8,4},{12,8},{16,12},{20,16},{24,20},{28,24},{5,1},{9,5},{13... | collective-permute-start | bytes 7077896 | tf_op jit(solution)/shard_map/ppermute | solution.py:99
  219.9 41.1 %collective-permute-start.9 = (f32[1,2,576,128]{3,2,1,0:T(8,128)}, f32[1,2,576,128]{3,2,1,0:T(8,128)}, u32[]{:S(2)}, u32[]{:S(2)}) collective-permute-start(f32[1,2,576,128]{3,2,1,0:T(8,128)} %get-tuple-element.27), channel_id=1, source_target_pairs={{0,2},{1,3},{2,0},{3,1},{4,6},{5,7},{6,4},{7,5},{8,10},{9,11},{10,... | collective-permute-start | bytes 1769480 | tf_op jit(solution)/shard_map/ppermute | solution.py:78
  221.3 39.7 %collective-permute-start.8 = (f32[1,2,576,128]{3,2,1,0:T(8,128)}, f32[1,2,576,128]{3,2,1,0:T(8,128)}, u32[]{:S(2)}, u32[]{:S(2)}) collective-permute-start(f32[1,2,576,128]{3,2,1,0:T(8,128)} %get-tuple-element.28), channel_id=1, source_target_pairs={{0,1},{1,2},{2,3},{3,0},{4,5},{5,6},{6,7},{7,4},{8,9},{9,10},{10,1... | collective-permute-start | bytes 1769480 | tf_op jit(solution)/shard_map/ppermute | solution.py:78
  222.7 38.3 %collective-permute-start.10 = (f32[1,2,576,128]{3,2,1,0:T(8,128)}, f32[1,2,576,128]{3,2,1,0:T(8,128)}, u32[]{:S(2)}, u32[]{:S(2)}) collective-permute-start(f32[1,2,576,128]{3,2,1,0:T(8,128)} %get-tuple-element.29), channel_id=1, source_target_pairs={{0,3},{1,0},{2,1},{3,2},{4,7},{5,4},{6,5},{7,6},{8,11},{9,8},{10,9... | collective-permute-start | bytes 1769480 | tf_op jit(solution)/shard_map/ppermute | solution.py:78
  226.3 34.7 %copy-start.3 = (f32[1,576,2,128]{3,1,2,0:T(8,128)S(1)}, f32[1,576,2,128]{3,1,2,0:T(8,128)}, u32[]{:S(2)}) copy-start(f32[1,576,2,128]{3,1,2,0:T(8,128)} %get-tuple-element.36) | copy-start | bytes 1769476
  301.5 8.6 %collective-permute-start.14 = (f32[]{:T(128)}, f32[]{:T(128)}, u32[]{:S(2)}, u32[]{:S(2)}) collective-permute-start(f32[]{:T(128)} %get-tuple-element.2), channel_id=1, source_target_pairs={{0,4},{4,8},{8,12},{12,16},{16,20},{20,24},{24,28},{28,0},{1,5},{5... | collective-permute-start | bytes 20 | tf_op jit(solution)/shard_map/ppermute | solution.py:48
  311.4 17.1 %collective-permute-start.15 = (f32[]{:T(128)}, f32[]{:T(128)}, u32[]{:S(2)}, u32[]{:S(2)}) collective-permute-start(f32[]{:T(128)} %max.15), channel_id=1, source_target_pairs={{0,8},{4,12},{8,16},{12,20},{16,24},{20,28},{24,0},{28,4},{1,9},{5... | collective-permute-start | bytes 20 | tf_op jit(solution)/shard_map/ppermute | solution.py:48
  329.2 6.1 %collective-permute-start.16 = (f32[]{:T(128)}, f32[]{:T(128)}, u32[]{:S(2)}, u32[]{:S(2)}) collective-permute-start(f32[]{:T(128)} %max.16), channel_id=1, source_target_pairs={{0,16},{4,20},{8,24},{12,28},{16,0},{20,4},{24,8},{28,12},{1,17},{... | collective-permute-start | bytes 20 | tf_op jit(solution)/shard_map/ppermute | solution.py:48
  336.0 5.3 %collective-permute-start.17 = (f32[]{:T(128)}, f32[]{:T(128)}, u32[]{:S(2)}, u32[]{:S(2)}) collective-permute-start(f32[]{:T(128)} %max.17), channel_id=1, source_target_pairs={{0,1},{1,2},{2,3},{3,0},{4,5},{5,6},{6,7},{7,4},{8,9},{9,10},{10,1... | collective-permute-start | bytes 20 | tf_op jit(solution)/shard_map/ppermute | solution.py:48
  342.0 4.5 %collective-permute-start.18 = (f32[]{:T(128)}, f32[]{:T(128)}, u32[]{:S(2)}, u32[]{:S(2)}) collective-permute-start(f32[]{:T(128)} %max.18), channel_id=1, source_target_pairs={{0,2},{1,3},{2,0},{3,1},{4,6},{5,7},{6,4},{7,5},{8,10},{9,11},{10,... | collective-permute-start | bytes 20 | tf_op jit(solution)/shard_map/ppermute | solution.py:48
  (5 other events, 19.1 us)
where the time goes:
time: 364 us; the launch traced here: 358 us
  waiting for transfers between devices  116 us (32%)
  starting transfers between devices  112 us (31%)
  matrix products  86.9 us (24%)
  other arithmetic  22.8 us (6%)
  local copies, waits for them, and re-layouts  13.7 us (4%)
  between operations  6.43 us (2%)
    ppermute x12, waiting for transfers between devices, exchange(): lax.ppermute(block, 'pa', [(i, (i + shift) % parts) for i in range(parts)])  105 us
    ppermute x12, starting transfers between devices, exchange(): lax.ppermute(block, 'pa', [(i, (i + shift) % parts) for i in range(parts)])  78.8 us
    dot_general x6, matrix products, to_x(): jnp.einsum('...zm,mx->...zx', flat, table_x, precision=lax.Precision.HIGH...  50.5 us
    dot_general x4, matrix products, exchange(): jnp.einsum('dnk,fjmk->dfjnm', table, modes, precision=lax.Precision.HIGH,...  36.4 us
    ppermute x5, starting transfers between devices, everywhere_max(): value = jnp.maximum(value, lax.ppermute(value, axis, pairs))  30.3 us
    ppermute x5, waiting for transfers between devices, everywhere_max(): value = jnp.maximum(value, lax.ppermute(value, axis, pairs))  11.3 us
    div x1, other arithmetic, body(): return (lamb / (magnitude + 1e-06), magnitude)  9.39 us
  transfers between devices with their start and end apart: 19, of which 8 were waited for; matrix products, arithmetic and copies ran while one was open for 17% of the time, Pallas kernels for 0%

commit v1 on v0

--- a/solution.py
+++ b/solution.py
@@ -1,15 +1,21 @@
+import functools
 import math
 
+import ml_dtypes
 import numpy as np
 
 import jax
 import jax.numpy as jnp
 from jax import lax
+from jax.experimental import pallas as pl
+from jax.experimental.pallas import tpu as pltpu
 from jax.sharding import PartitionSpec as P
 
 NX = 1536
 NZ = 1152
 KX = 512
+MESH = pl.DeviceIdType.MESH
+TILE = 256
 
 
 def z_table(length, modes, parts):
@@ -50,7 +56,7 @@
     return value
 
 
-def body(spectral_velocity, inverse_spacing):
+def plain_body(spectral_velocity, inverse_spacing):
     planes, kx_local, width = spectral_velocity.shape[1:]
     parts = lax.axis_size("pa")
     levels = lax.axis_size("gy")
@@ -115,6 +121,419 @@
     return (lamb / (magnitude + 1e-06), magnitude)
 
 
+def halves(table):
+    table = np.asarray(table, np.float32)
+    high = table.astype(ml_dtypes.bfloat16)
+    low = (table - high.astype(np.float32)).astype(ml_dtypes.bfloat16)
+    return high, low
+
+
+def z_factors(length, modes, parts):
+    slab = length // parts
+    half = slab // 2
+    top = modes // 2
+    middle = (slab - 1) / 2
+    points = np.arange(half, slab) - middle
+    wave = np.arange(top + 1)
+    step = 2.0 * math.pi / length
+    angle = step * np.outer(points, wave)
+    share = wave / top
+    even = np.concatenate((np.cos(angle), -share * np.sin(angle)))
+    odd = np.concatenate((np.sin(angle), share * np.cos(angle)))
+    left_e, size_e, _ = np.linalg.svd(even, full_matrices=False)
+    left_o, size_o, _ = np.linalg.svd(odd, full_matrices=False)
+    limit = 3e-8 * max(size_e[0], size_o[0])
+    rank = max(int((size_e > limit).sum()), int((size_o > limit).sum()))
+    rank = min(-(-rank // 4) * 4, size_e.size, size_o.size)
+    left_e, left_o = left_e[:, :rank], left_o[:, :rank]
+    value = np.concatenate((
+        np.concatenate((left_e[:half][::-1], left_e[:half])),
+        np.concatenate((-left_o[:half][::-1], left_o[:half])),
+    ), 1)
+    slope = np.concatenate((
+        np.concatenate((-left_e[half:][::-1], left_e[half:])),
+        np.concatenate((left_o[half:][::-1], left_o[half:])),
+    ), 1) * (top * step)
+    column = np.arange(modes)
+    signed = np.where(column < top, column, column - modes)
+    kernel = np.concatenate((
+        (left_e.T @ even)[:, np.abs(signed)] + 0j,
+        1j * np.sign(signed) * (left_o.T @ odd)[:, np.abs(signed)],
+    ))
+    centre = np.arange(parts) * slab + middle
+    phase = np.exp(1j * step * np.outer(centre, signed))
+    return np.concatenate((value, slope)), kernel[None] * phase[:, None, :]
+
+
+def z_tables(length, modes, parts):
+    expand, reduce = z_factors(length, modes, parts)
+    rank = expand.shape[1]
+    real = np.concatenate((reduce.real, -reduce.imag), 2)
+    imag = np.concatenate((reduce.imag, reduce.real), 2)
+    table = np.concatenate((real, imag), 1)
+    reduce = np.concatenate(halves(table), 1)
+    wide = np.zeros((expand.shape[0], -(-rank // TILE) * TILE), np.float32)
+    wide[:, :rank] = expand
+    return reduce, np.stack(halves(wide)), rank
+
+
+def x_tables(length, modes):
+    column = np.arange(modes)
+    angle = (column[:, None] * np.arange(length)[None, :] % length) * (2.0 * math.pi / length)
+    weight = np.where(column == 0, 1.0, 2.0)[:, None]
+    return np.stack(halves(np.concatenate((weight * np.cos(angle), -weight * np.sin(angle)))))
+
+
+def split(value):
+    high = value.astype(jnp.bfloat16)
+    return high, (value - high.astype(jnp.float32)).astype(jnp.bfloat16)
+
+
+def dot(a, b):
+    return jnp.dot(a, b, preferred_element_type=jnp.float32)
+
+
+def field_kernel(
+    parts, levels, rank, wave_ref, space_ref, x_hbm, reduce_hbm, expand_hbm, table_hbm,
+    lamb_ref, peak_ref,
+    x_ref, xt_ref, reduce_ref, expand_ref, table_ref, send, recv, halo, lhs, part_x, peaks,
+    load_sem, send_sem, recv_sem, halo_send, halo_recv, peak_send, peak_recv,
+):
+    me, level = lax.axis_index("pa"), lax.axis_index("gy")
+    planes, kx_local, width = x_ref.shape[1:]
+    slab = lamb_ref.shape[2]
+    two = 2 * rank
+    tall = lhs.shape[0] // 4
+    wide = expand_ref.shape[2]
+    shifts = sorted(range(1, parts), key=lambda s: (abs(2 * s - parts), s))
+    fields = (0, 2, 1)
+
+    loads = {}
+
+    def load(key, source, target):
+        loads[key] = pltpu.make_async_copy(source, target, load_sem.at[len(loads)])
+        loads[key].start()
+
+    def slab_of(shift):
+        return lax.rem(me + shift, parts)
+
+    load(("x", 0), x_hbm.at[0], x_ref.at[0])
+    for shift in shifts + [0]:
+        load(("reduce", shift), reduce_hbm.at[slab_of(shift)], reduce_ref.at[shift])
+    load(("x", 2), x_hbm.at[2], x_ref.at[2])
+    load(("x", 1), x_hbm.at[1], x_ref.at[1])
+    load("table", table_hbm, table_ref)
+    load("expand", expand_hbm, expand_ref)
+
+    @pl.when(level == 0)
+    def _():
+        halo[:, 0] = jnp.zeros_like(halo[:, 0])
+
+    @pl.when(level == levels - 1)
+    def _():
+        halo[:, 1] = jnp.zeros_like(halo[:, 1])
+
+    barrier = pltpu.get_barrier_semaphore()
+    for shift in range(1, parts):
+        pl.semaphore_signal(
+            barrier, inc=1, device_id={"pa": slab_of(shift)}, device_id_type=MESH
+        )
+    for shift in range(1, levels):
+        pl.semaphore_signal(
+            barrier, inc=1, device_id={"gy": lax.rem(level + shift, levels)}, device_id_type=MESH
+        )
+    pl.semaphore_wait(barrier, parts + levels - 2)
+
+    def transfer(f, j, shift):
+        return pltpu.make_async_remote_copy(
+            src_ref=send.at[f, j, shift - 1],
+            dst_ref=recv.at[f, j, me],
+            send_sem=send_sem.at[f, j, shift],
+            recv_sem=recv_sem.at[f, j, shift],
+            device_id={"pa": slab_of(shift)},
+            device_id_type=MESH,
+        )
+
+    def arrive(f, j):
+        for shift in shifts:
+            transfer(f, j, shift).wait_recv()
+
+    def reduce_field(f):
+        loads["x", f].wait()
+
+        @pl.loop(0, width // 128)
+        def _(n):
+            at = pl.ds(pl.multiple_of(n * 128, 128), 128)
+            for j in range(planes):
+                high, low = split(x_ref[f, j, :, at].T)
+                lanes = slice(j * kx_local, (j + 1) * kx_local)
+                xt_ref[0, at, lanes] = high
+                xt_ref[1, at, lanes] = low
+
+        for shift in shifts + [0]:
+            if f == fields[0]:
+                loads["reduce", shift].wait()
+            both = dot(reduce_ref[shift], xt_ref[0])
+            out = both[:two] + both[two:] + dot(reduce_ref[shift, :two, :], xt_ref[1])
+            for j in range(planes):
+                piece = out[:, j * kx_local : (j + 1) * kx_local]
+                if shift:
+                    send[f, j, shift - 1] = piece
+                else:
+                    recv[f, j, me] = piece
+            if shift:
+                for j in range(planes):
+                    transfer(f, j, shift).start()
+
+    def halo_copy(f, up):
+        if up:
+            return pltpu.make_async_remote_copy(
+                src_ref=recv.at[f, planes - 1], dst_ref=halo.at[f // 2, 0],
+                send_sem=halo_send.at[f // 2, 0], recv_sem=halo_recv.at[f // 2, 0],
+                device_id={"gy": lax.rem(level + 1, levels)}, device_id_type=MESH,
+            )
+        return pltpu.make_async_remote_copy(
+            src_ref=recv.at[f, 0], dst_ref=halo.at[f // 2, 1],
+            send_sem=halo_send.at[f // 2, 1], recv_sem=halo_recv.at[f // 2, 1],
+            device_id={"gy": lax.rem(level + levels - 1, levels)}, device_id_type=MESH,
+        )
+
+    def halo_start(f):
+        @pl.when(level < levels - 1)
+        def _():
+            halo_copy(f, True).start()
+
+        @pl.when(level > 0)
+        def _():
+            halo_copy(f, False).start()
+
+    def halo_arrive(f):
+        @pl.when(level > 0)
+        def _():
+            halo_copy(f, True).wait_recv()
+
+        @pl.when(level < levels - 1)
+        def _():
+            halo_copy(f, False).wait_recv()
+
+    def halo_sent(f):
+        @pl.when(level < levels - 1)
+        def _():
+            halo_copy(f, True).wait_send()
+
+        @pl.when(level > 0)
+        def _():
+            halo_copy(f, False).wait_send()
+
+    def fill(slot, hat):
+        @pl.loop(0, parts)
+        def _(source):
+            here = pl.multiple_of(source * kx_local, kx_local)
+            for c in range(2):
+                value = hat(source, here, c)
+                if tall > rank:
+                    value = jnp.concatenate((value, jnp.zeros((tall - rank, kx_local), jnp.float32)))
+                high, low = split(value)
+                lanes = pl.ds(pl.multiple_of(c * KX + here, kx_local), kx_local)
+                lhs[slot * tall : (slot + 1) * tall, lanes] = high
+                lhs[(2 + slot) * tall : (3 + slot) * tall, lanes] = low
+
+    def half(c):
+        return slice(c * rank, (c + 1) * rank)
+
+    def modes(f, j):
+        return lambda source, here, c: recv[f, j, source, half(c), :]
+
+    def turned(f, j):
+        def hat(source, here, c):
+            wave = wave_ref[0:1, pl.ds(here, kx_local)]
+            other = recv[f, j, source, half(1 - c), :] * wave
+            return other if c else -other
+        return hat
+
+    def slope_y(f, j):
+        def hat(source, here, c):
+            lower = halo[f // 2, 0, source, half(c), :] if j == 0 else recv[f, j - 1, source, half(c), :]
+            upper = (
+                halo[f // 2, 1, source, half(c), :] if j == planes - 1
+                else recv[f, j + 1, source, half(c), :]
+            )
+            return (upper - lower) * space_ref[j]
+        return hat
+
+    def minus(first, second):
+        return lambda source, here, c: first(source, here, c) - second(source, here, c)
+
+    def to_x(at):
+        both = dot(lhs[...], table_ref[0, :, at])
+        out = both[: 2 * tall] + both[2 * tall :] + dot(lhs[: 2 * tall, :], table_ref[1, :, at])
+        return out[:tall], out[tall:]
+
+    def to_z(value, rows):
+        if wide > tall:
+            value = jnp.concatenate((value, jnp.zeros((wide - tall, TILE), jnp.float32)))
+        high, low = split(value)
+        return (
+            dot(expand_ref[0, :rows, :], high)
+            + dot(expand_ref[1, :rows, :], high)
+            + dot(expand_ref[0, :rows, :], low)
+        )
+
+    def tiles(step, init):
+        def at_tile(t, carry):
+            return step(pl.ds(pl.multiple_of(t * TILE, TILE), TILE), carry)
+        return lax.fori_loop(0, NX // TILE, at_tile, init)
+
+    for f in fields:
+        reduce_field(f)
+    loads["table"].wait()
+    loads["expand"].wait()
+
+    for j in range(planes):
+        arrive(0, j)
+    halo_start(0)
+    for j in range(planes):
+        fill(j, modes(0, j))
+
+    def u_tile(at, carry):
+        for j, value in enumerate(to_x(at)):
+            both = to_z(value, 2 * slab)
+            lamb_ref[0, j, :, at] = both[:slab]
+            lamb_ref[2, j, :, at] = both[slab:]
+        return carry
+
+    tiles(u_tile, 0)
+
+    for j in range(planes):
+        arrive(2, j)
+    halo_start(2)
+    for j in range(planes):
+        fill(0, modes(2, j))
+        fill(1, turned(2, j))
+
+        def w_tile(at, carry):
+            w, dx_w = to_x(at)
+            lamb_ref[1, j, :, at] = to_z(w, slab)
+            lamb_ref[2, j, :, at] = lamb_ref[2, j, :, at] - to_z(dx_w, slab)
+            return carry
+
+        tiles(w_tile, 0)
+
+    halo_arrive(0)
+    halo_arrive(2)
+    for j in range(planes):
+        fill(j, slope_y(2, j))
+
+    def dy_tile(at, carry):
+        for j, value in enumerate(to_x(at)):
+            part_x[j, :, at] = to_z(value, slab)
+        return carry
+
+    tiles(dy_tile, 0)
+
+    top = jnp.zeros((8, TILE), jnp.float32)
+    for j in range(planes):
+        arrive(1, j)
+        fill(0, modes(1, j))
+        fill(1, minus(turned(1, j), slope_y(0, j)))
+
+        def v_tile(at, top):
+            v, vort_z = to_x(at)
+            v = to_z(v, 2 * slab)
+            vort_z = to_z(vort_z, slab)
+            vort_x = part_x[j, :, at] - v[slab:]
+            v = v[:slab]
+            u, w, vort_y = lamb_ref[0, j, :, at], lamb_ref[1, j, :, at], lamb_ref[2, j, :, at]
+            lamb_ref[0, j, :, at] = v * vort_z - w * vort_y
+            lamb_ref[1, j, :, at] = w * vort_x - u * vort_z
+            lamb_ref[2, j, :, at] = u * vort_y - v * vort_x
+            square = vort_x * vort_x + vort_y * vort_y + vort_z * vort_z
+            return jnp.maximum(top, square.reshape(slab // 8, 8, TILE).max(0))
+
+        top = tiles(v_tile, top)
+
+    def peak_copy(axis, count, base, here, shift):
+        return pltpu.make_async_remote_copy(
+            src_ref=peaks.at[base], dst_ref=peaks.at[base + shift],
+            send_sem=peak_send.at[base + shift], recv_sem=peak_recv.at[base + shift],
+            device_id={axis: lax.rem(here + shift, count)}, device_id_type=MESH,
+        )
+
+    value = top[:, :128]
+    for k in range(1, TILE // 128):
+        value = jnp.maximum(value, top[:, k * 128 : (k + 1) * 128])
+    base = 0
+    for axis, count, here in (("gy", levels, level), ("pa", parts, me)):
+        peaks[base] = value
+        copies = [peak_copy(axis, count, base, here, shift) for shift in range(1, count)]
+        for copy in copies:
+            copy.start()
+        for copy in copies:
+            copy.wait()
+        for shift in range(1, count):
+            value = jnp.maximum(value, peaks[base + shift])
+        base += count
+    peak = jnp.sqrt(jnp.max(value, axis=(0, 1), keepdims=True))
+    peak_ref[0] = jnp.broadcast_to(peak, value.shape)
+    peak_ref[1] = jnp.broadcast_to(1.0 / (peak + 1e-06), value.shape)
+
+    for f in fields:
+        for j in range(planes):
+            for shift in shifts:
+                transfer(f, j, shift).wait_send()
+    halo_sent(0)
+    halo_sent(2)
+
+
+def body(spectral_velocity, inverse_spacing):
+    planes, kx_local, width = spectral_velocity.shape[1:]
+    parts, levels = lax.axis_size("pa"), lax.axis_size("gy")
+    slab = NZ // parts
+    if planes != 2 or kx_local % 128 or slab % 16 or parts < 2 or levels < 2:
+        return plain_body(spectral_velocity, inverse_spacing)
+    reduce, expand, rank = z_tables(NZ, width // 2, parts)
+    table = x_tables(NX, KX)
+    wave = np.tile((np.arange(KX) * (2.0 * math.pi / NX)).astype(np.float32), (8, 1))
+    tall = -(-rank // 16) * 16
+    hbm = pl.BlockSpec(memory_space=pl.ANY)
+    vmem = pl.BlockSpec(memory_space=pltpu.VMEM)
+    block = (parts, 2 * rank, kx_local)
+    dma = pltpu.SemaphoreType.DMA
+    lamb, peak = pl.pallas_call(
+        functools.partial(field_kernel, parts, levels, rank),
+        out_shape=(
+            jax.ShapeDtypeStruct((3, planes, slab, NX), jnp.float32),
+            jax.ShapeDtypeStruct((2, 8, 128), jnp.float32),
+        ),
+        in_specs=[vmem, pl.BlockSpec(memory_space=pltpu.SMEM), hbm, hbm, hbm, hbm],
+        out_specs=(vmem, vmem),
+        scratch_shapes=[
+            pltpu.VMEM((3, planes, kx_local, width), jnp.float32),
+            pltpu.VMEM((2, width, planes * kx_local), jnp.bfloat16),
+            pltpu.VMEM(reduce.shape, jnp.bfloat16),
+            pltpu.VMEM(expand.shape, jnp.bfloat16),
+            pltpu.VMEM(table.shape, jnp.bfloat16),
+            pltpu.VMEM((3, planes, parts - 1) + block[1:], jnp.float32),
+            pltpu.VMEM((3, planes) + block, jnp.float32),
+            pltpu.VMEM((2, 2) + block, jnp.float32),
+            pltpu.VMEM((4 * tall, 2 * KX), jnp.bfloat16),
+            pltpu.VMEM((planes, slab, NX), jnp.float32),
+            pltpu.VMEM((parts + levels, 8, 128), jnp.float32),
+            dma((parts + 5,)),
+            dma((3, planes, parts)),
+            dma((3, planes, parts)),
+            dma((2, 2)),
+            dma((2, 2)),
+            dma((parts + levels,)),
+            dma((parts + levels,)),
+        ],
+        compiler_params=pltpu.CompilerParams(
+            collective_id=0, has_side_effects=True, vmem_limit_bytes=62 * 2**20
+        ),
+    )(wave, inverse_spacing, spectral_velocity, reduce, expand, table)
+    return lamb * peak[1, 0, 0], peak[0, 0, 0]
+
+
 def solution(mesh):
     placed = (P(None, "gy", "pa", None), P("gy"))
     return jax.shard_map(

time: 364 us -> 188 us (0.52); the launches traced: 358 us -> 187 us
  Pallas kernels: 0 us -> 175 us
  waiting for transfers between devices: 116 us -> 0 us
  starting transfers between devices: 112 us -> 0 us
  matrix products: 86.9 us -> 0 us
  local copies, waits for them, and re-layouts: 13.7 us -> 1.21 us
  other arithmetic: 22.8 us -> 10.7 us
  between operations: 6.43 us -> 0.64 us
    pallas_call x0 -> x1, Pallas kernels: none -> 175 us  [body(): pl.pallas_call(functools.partial(field_kernel, parts, levels, rank), out_...]
    ppermute x19 -> x0, waiting for transfers between devices: 116 us -> none  [the longest x12 105 us: exchange(): lax.ppermute(block, 'pa', [(i, (i + shift) % parts) for i in range(parts)])]
    ppermute x19 -> x0, starting transfers between devices: 112 us -> none  [the longest x12 78.8 us: exchange(): lax.ppermute(block, 'pa', [(i, (i + shift) % parts) for i in range(parts)])]
    dot_general x10 -> x0, matrix products: 86.9 us -> none  [the longest x6 50.5 us: to_x(): jnp.einsum('...zm,mx->...zx', flat, table_x, precision=lax.Precision.HIGH...]
    div x1 -> x0, other arithmetic: 9.39 us -> none  [body(): return (lamb / (magnitude + 1e-06), magnitude)]
    unnamed x24 -> x0, local copies, waits for them, and re-layouts: 6.45 us -> none
    mul x4 -> x1, other arithmetic: 4.43 us -> 10.7 us  [body(): return (lamb * peak[1, 0, 0], peak[0, 0, 0])]
    concatenate x3 -> x0, other arithmetic: 6.02 us -> none  [exchange(): whole = jnp.concatenate(got, axis=-1)]
  transfers between devices with their start and end apart: 19 -> 0, of which waited for: 8 -> 0; matrix products, arithmetic and copies ran while one was open for 17% -> 0% of each run, Pallas kernels for 0% -> 0%
where the time goes in v1:
time: 188 us; the launch traced here: 187 us
  Pallas kernels  175 us (93%)
  other arithmetic  10.7 us (6%)
    pallas_call x1, Pallas kernels, body(): pl.pallas_call(functools.partial(field_kernel, parts, levels, rank), out_...  175 us
    mul x1, other arithmetic, body(): return (lamb * peak[1, 0, 0], peak[0, 0, 0])  10.7 us

profile of v1, /device:TPU:0, one launch (start us, length us, event | category | flops | bytes accessed | tf_op | source)
XLA Modules:
  0.0 187.5 jit_solution(3840620121993570731)
XLA Ops:
  0.6 174.9 %shard_map.77 = (f32[3,2,288,1536]{3,2,1,0:T(8,128)}, f32[2,8,128]{2,1,0:T(8,128)}) custom-call(f32[8,512]{1,0:T(8,128)} %constant.8.clone.wave_ref, f32[2]{0:T(128)} %space_ref.1, f32[3,2,128,1536]{3,2,1,0:T(8,128)} %x_hbm.1, bf16[4,864,1536]{2,1,0:T(8,128)(2,1)} %constant.9.clone.reduce_hbm, bf16[2,576,256]{2,1,0:T(8,128)(2,1)} %constant.10.clone.expand_hbm, ...), custom_call_target="tpu_custom_call" | custom-call | tf_op jit(solution)/shard_map/pallas_call | solution.py:502
  175.5 1.2 fusion
  176.8 10.7 %broadcast_multiply_fusion = f32[3,2,288,1536]{3,2,1,0:T(8,128)} fusion(f32[3,2,288,1536]{3,2,1,0:T(8,128)} %get-tuple-element.4, f32[]{:T(128)} %bitcast), kind=kLoop, calls=%fused_computation | loop fusion | flops 2654208 | bytes 21233668 | tf_op jit(solution)/shard_map/mul | solution.py:534

commit v2 on v1

--- a/solution.py
+++ b/solution.py
@@ -177,11 +177,18 @@
     return reduce, np.stack(halves(wide)), rank
 
 
-def x_tables(length, modes):
-    column = np.arange(modes)
-    angle = (column[:, None] * np.arange(length)[None, :] % length) * (2.0 * math.pi / length)
-    weight = np.where(column == 0, 1.0, 2.0)[:, None]
-    return np.stack(halves(np.concatenate((weight * np.cos(angle), -weight * np.sin(angle)))))
+def x_tables(length, modes, parts):
+    own = modes // parts
+    column = np.arange(modes).reshape(parts, own // 2, 2).transpose(2, 0, 1)[:, :, None, :]
+    step = 2.0 * math.pi / length
+    angle = (column[..., None] * np.arange(length // 2) % length) * step
+    weight = np.where(column == 0, 1.0, 2.0)[..., None]
+    table = np.concatenate((weight * np.cos(angle), -weight * np.sin(angle)), 2)
+    wave = np.concatenate((-step * column, step * column), 2).reshape(2, 1, modes)
+    return (
+        np.stack(halves(table.reshape(2, modes, length // 2))),
+        np.tile(wave.astype(np.float32), (1, 8, 1)),
+    )
 
 
 def split(value):
@@ -196,7 +203,7 @@
 def field_kernel(
     parts, levels, rank, wave_ref, space_ref, x_hbm, reduce_hbm, expand_hbm, table_hbm,
     lamb_ref, peak_ref,
-    x_ref, xt_ref, reduce_ref, expand_ref, table_ref, send, recv, halo, lhs, part_x, peaks,
+    x_ref, xt_ref, reduce_ref, expand_ref, table_ref, send, recv, halo, lhs, part_x, peaks, tile,
     load_sem, send_sem, recv_sem, halo_send, halo_recv, peak_send, peak_recv,
 ):
     me, level = lax.axis_index("pa"), lax.axis_index("gy")
@@ -265,7 +272,12 @@
         def _(n):
             at = pl.ds(pl.multiple_of(n * 128, 128), 128)
             for j in range(planes):
-                high, low = split(x_ref[f, j, :, at].T)
+                tile[j] = x_ref[f, j, :, at]
+                rows = jnp.concatenate((
+                    tile[j, pl.ds(0, kx_local // 2, stride=2), :],
+                    tile[j, pl.ds(1, kx_local // 2, stride=2), :],
+                ))
+                high, low = split(rows.T)
                 lanes = slice(j * kx_local, (j + 1) * kx_local)
                 xt_ref[0, at, lanes] = high
                 xt_ref[1, at, lanes] = low
@@ -276,14 +288,26 @@
             both = dot(reduce_ref[shift], xt_ref[0])
             out = both[:two] + both[two:] + dot(reduce_ref[shift, :two, :], xt_ref[1])
             for j in range(planes):
-                piece = out[:, j * kx_local : (j + 1) * kx_local]
+                real = out[:rank, j * kx_local : (j + 1) * kx_local]
+                imag = out[rank:, j * kx_local : (j + 1) * kx_local]
+                first = lax.broadcasted_iota(jnp.int32, real.shape, 1) < kx_local // 2
+                even = jnp.where(first, real, pltpu.roll(imag, kx_local // 2, 1))
+                odd = jnp.where(first, pltpu.roll(real, kx_local // 2, 1), imag)
                 if shift:
-                    send[f, j, shift - 1] = piece
+                    send[f, j, shift - 1, half(0), :] = even
+                    send[f, j, shift - 1, half(1), :] = odd
                 else:
-                    recv[f, j, me] = piece
-            if shift:
+                    recv[f, j, me, half(0), :] = even
+                    recv[f, j, me, half(1), :] = odd
+            if shift and f == fields[0]:
                 for j in range(planes):
                     transfer(f, j, shift).start()
+
+    def follow(f, before):
+        for j in range(planes):
+            for shift in shifts:
+                transfer(before, j, shift).wait_send()
+                transfer(f, j, shift).start()
 
     def halo_copy(f, up):
         if up:
@@ -346,9 +370,8 @@
 
     def turned(f, j):
         def hat(source, here, c):
-            wave = wave_ref[0:1, pl.ds(here, kx_local)]
-            other = recv[f, j, source, half(1 - c), :] * wave
-            return other if c else -other
+            wave = wave_ref[c, 0:1, pl.ds(here, kx_local)]
+            return pltpu.roll(recv[f, j, source, half(c), :], kx_local // 2, 1) * wave
         return hat
 
     def slope_y(f, j):
@@ -365,13 +388,18 @@
         return lambda source, here, c: first(source, here, c) - second(source, here, c)
 
     def to_x(at):
-        both = dot(lhs[...], table_ref[0, :, at])
-        out = both[: 2 * tall] + both[2 * tall :] + dot(lhs[: 2 * tall, :], table_ref[1, :, at])
+        def of(c):
+            lanes = slice(c * KX, (c + 1) * KX)
+            both = dot(lhs[:, lanes], table_ref[0, c, :, at])
+            return both[: 2 * tall] + both[2 * tall :] + dot(lhs[: 2 * tall, lanes], table_ref[1, c, :, at])
+
+        even, odd = of(0), of(1)
+        out = jnp.concatenate((even + odd, even - odd), 1)
         return out[:tall], out[tall:]
 
     def to_z(value, rows):
         if wide > tall:
-            value = jnp.concatenate((value, jnp.zeros((wide - tall, TILE), jnp.float32)))
+            value = jnp.concatenate((value, jnp.zeros((wide - tall, 2 * TILE), jnp.float32)))
         high, low = split(value)
         return (
             dot(expand_ref[0, :rows, :], high)
@@ -381,29 +409,34 @@
 
     def tiles(step, init):
         def at_tile(t, carry):
-            return step(pl.ds(pl.multiple_of(t * TILE, TILE), TILE), carry)
-        return lax.fori_loop(0, NX // TILE, at_tile, init)
+            at = pl.ds(pl.multiple_of(t * TILE, TILE), TILE)
+            far = pl.ds(pl.multiple_of(NX // 2 + t * TILE, TILE), TILE)
+            return step(at, ((slice(0, TILE), at), (slice(TILE, 2 * TILE), far)), carry)
+        return lax.fori_loop(0, NX // 2 // TILE, at_tile, init)
 
     for f in fields:
         reduce_field(f)
     loads["table"].wait()
     loads["expand"].wait()
 
+    follow(2, 0)
     for j in range(planes):
         arrive(0, j)
     halo_start(0)
     for j in range(planes):
         fill(j, modes(0, j))
 
-    def u_tile(at, carry):
+    def u_tile(at, sides, carry):
         for j, value in enumerate(to_x(at)):
             both = to_z(value, 2 * slab)
-            lamb_ref[0, j, :, at] = both[:slab]
-            lamb_ref[2, j, :, at] = both[slab:]
+            for part, to in sides:
+                lamb_ref[0, j, :, to] = both[:slab, part]
+                lamb_ref[2, j, :, to] = both[slab:, part]
         return carry
 
     tiles(u_tile, 0)
 
+    follow(1, 2)
     for j in range(planes):
         arrive(2, j)
     halo_start(2)
@@ -411,10 +444,12 @@
         fill(0, modes(2, j))
         fill(1, turned(2, j))
 
-        def w_tile(at, carry):
+        def w_tile(at, sides, carry):
             w, dx_w = to_x(at)
-            lamb_ref[1, j, :, at] = to_z(w, slab)
-            lamb_ref[2, j, :, at] = lamb_ref[2, j, :, at] - to_z(dx_w, slab)
+            w, dx_w = to_z(w, slab), to_z(dx_w, slab)
+            for part, to in sides:
+                lamb_ref[1, j, :, to] = w[:, part]
+                lamb_ref[2, j, :, to] = lamb_ref[2, j, :, to] - dx_w[:, part]
             return carry
 
         tiles(w_tile, 0)
@@ -424,9 +459,11 @@
     for j in range(planes):
         fill(j, slope_y(2, j))
 
-    def dy_tile(at, carry):
+    def dy_tile(at, sides, carry):
         for j, value in enumerate(to_x(at)):
-            part_x[j, :, at] = to_z(value, slab)
+            value = to_z(value, slab)
+            for part, to in sides:
+                part_x[j, :, to] = value[:, part]
         return carry
 
     tiles(dy_tile, 0)
@@ -437,18 +474,20 @@
         fill(0, modes(1, j))
         fill(1, minus(turned(1, j), slope_y(0, j)))
 
-        def v_tile(at, top):
-            v, vort_z = to_x(at)
-            v = to_z(v, 2 * slab)
-            vort_z = to_z(vort_z, slab)
-            vort_x = part_x[j, :, at] - v[slab:]
-            v = v[:slab]
-            u, w, vort_y = lamb_ref[0, j, :, at], lamb_ref[1, j, :, at], lamb_ref[2, j, :, at]
-            lamb_ref[0, j, :, at] = v * vort_z - w * vort_y
-            lamb_ref[1, j, :, at] = w * vort_x - u * vort_z
-            lamb_ref[2, j, :, at] = u * vort_y - v * vort_x
-            square = vort_x * vort_x + vort_y * vort_y + vort_z * vort_z
-            return jnp.maximum(top, square.reshape(slab // 8, 8, TILE).max(0))
+        def v_tile(at, sides, top):
+            value, turn = to_x(at)
+            value = to_z(value, 2 * slab)
+            turn = to_z(turn, slab)
+            for part, to in sides:
+                v, vort_z = value[:slab, part], turn[:, part]
+                vort_x = part_x[j, :, to] - value[slab:, part]
+                u, w, vort_y = lamb_ref[0, j, :, to], lamb_ref[1, j, :, to], lamb_ref[2, j, :, to]
+                lamb_ref[0, j, :, to] = v * vort_z - w * vort_y
+                lamb_ref[1, j, :, to] = w * vort_x - u * vort_z
+                lamb_ref[2, j, :, to] = u * vort_y - v * vort_x
+                square = vort_x * vort_x + vort_y * vort_y + vort_z * vort_z
+                top = jnp.maximum(top, square.reshape(slab // 8, 8, TILE).max(0))
+            return top
 
         top = tiles(v_tile, top)
 
@@ -474,13 +513,20 @@
             value = jnp.maximum(value, peaks[base + shift])
         base += count
     peak = jnp.sqrt(jnp.max(value, axis=(0, 1), keepdims=True))
-    peak_ref[0] = jnp.broadcast_to(peak, value.shape)
-    peak_ref[1] = jnp.broadcast_to(1.0 / (peak + 1e-06), value.shape)
-
-    for f in fields:
-        for j in range(planes):
-            for shift in shifts:
-                transfer(f, j, shift).wait_send()
+    scale = 1.0 / (peak + 1e-06)
+
+    @pl.loop(0, slab // 16)
+    def _(n):
+        rows = pl.ds(pl.multiple_of(n * 16, 16), 16)
+        for c in range(3):
+            for j in range(planes):
+                lamb_ref[c, j, rows, :] = lamb_ref[c, j, rows, :] * scale
+
+    peak_ref[...] = jnp.broadcast_to(peak, peak_ref.shape)
+
+    for j in range(planes):
+        for shift in shifts:
+            transfer(1, j, shift).wait_send()
     halo_sent(0)
     halo_sent(2)
 
@@ -492,8 +538,7 @@
     if planes != 2 or kx_local % 128 or slab % 16 or parts < 2 or levels < 2:
         return plain_body(spectral_velocity, inverse_spacing)
     reduce, expand, rank = z_tables(NZ, width // 2, parts)
-    table = x_tables(NX, KX)
-    wave = np.tile((np.arange(KX) * (2.0 * math.pi / NX)).astype(np.float32), (8, 1))
+    table, wave = x_tables(NX, KX, parts)
     tall = -(-rank // 16) * 16
     hbm = pl.BlockSpec(memory_space=pl.ANY)
     vmem = pl.BlockSpec(memory_space=pltpu.VMEM)
@@ -502,8 +547,8 @@
     lamb, peak = pl.pallas_call(
         functools.partial(field_kernel, parts, levels, rank),
         out_shape=(
-            jax.ShapeDtypeStruct((3, planes, slab, NX), jnp.float32),
-            jax.ShapeDtypeStruct((2, 8, 128), jnp.float32),
+            pltpu.VMEM((3, planes, slab, NX), jnp.float32),
+            jax.ShapeDtypeStruct((8, 128), jnp.float32),
         ),
         in_specs=[vmem, pl.BlockSpec(memory_space=pltpu.SMEM), hbm, hbm, hbm, hbm],
         out_specs=(vmem, vmem),
@@ -519,6 +564,7 @@
             pltpu.VMEM((4 * tall, 2 * KX), jnp.bfloat16),
             pltpu.VMEM((planes, slab, NX), jnp.float32),
             pltpu.VMEM((parts + levels, 8, 128), jnp.float32),
+            pltpu.VMEM((planes, kx_local, 128), jnp.float32),
             dma((parts + 5,)),
             dma((3, planes, parts)),
             dma((3, planes, parts)),
@@ -528,10 +574,10 @@
             dma((parts + levels,)),
         ],
         compiler_params=pltpu.CompilerParams(
-            collective_id=0, has_side_effects=True, vmem_limit_bytes=62 * 2**20
+            collective_id=0, has_side_effects=True, vmem_limit_bytes=51 * 2**20
         ),
     )(wave, inverse_spacing, spectral_velocity, reduce, expand, table)
-    return lamb * peak[1, 0, 0], peak[0, 0, 0]
+    return lamb, peak[0, 0]
 
 
 def solution(mesh):

time: 188 us -> 159 us (0.85)
  Pallas kernels: 175 us -> 153 us
  other arithmetic: 10.7 us -> 0 us
  local copies, waits for them, and re-layouts: 1.21 us -> 5.31 us
    pallas_call x1, Pallas kernels: 175 us -> 153 us  [body(): pl.pallas_call(functools.partial(field_kernel, parts, levels, rank), out_...]
    mul x1 -> x0, other arithmetic: 10.7 us -> none  [body(): return (lamb * peak[1, 0, 0], peak[0, 0, 0])]
    unnamed x0 -> x1, local copies, waits for them, and re-layouts: none -> 4.13 us
where the time goes in v2:
time: 159 us
  Pallas kernels  153 us (96%)
  local copies, waits for them, and re-layouts  5.31 us (3%)
    pallas_call x1, Pallas kernels, body(): pl.pallas_call(functools.partial(field_kernel, parts, levels, rank), out_...  153 us
    unnamed x1, local copies, waits for them, and re-layouts  4.13 us

profile of v2, /device:TPU:0, one launch (start us, length us, event | category | flops | bytes accessed | tf_op | source)
XLA Modules:
  0.0 158.6 jit_solution(14127411919506882728)
XLA Ops:
  0.6 152.7 %shard_map.77 = (f32[3,2,288,1536]{3,2,1,0:T(8,128)S(1)}, f32[8,128]{1,0:T(8,128)}) custom-call(f32[2,8,512]{2,1,0:T(8,128)} %constant.8.clone.wave_ref, f32[2]{0:T(128)} %space_ref.1, f32[3,2,128,1536]{3,2,1,0:T(8,128)} %x_hbm.1, bf16[4,864,1536]{2,1,0:T(8,128)(2,1)} %constant.9.clone.reduce_hbm, bf16[2,576,256]{2,1,0:T(8,128)(2,1)} %constant.10.clone.expand_hbm, ...), custom_call_target="tpu_custom_call" | custom-call | tf_op jit(solution)/shard_map/pallas_call | solution.py:547
  153.3 1.2 slice.3
  154.5 4.1 %copy.9 = f32[3,2,288,1536]{3,2,1,0:T(8,128)} copy(f32[3,2,288,1536]{3,2,1,0:T(8,128)S(1)} %get-tuple-element.6) | data formatting | bytes 21233664

commit v3 on v2

--- a/solution.py
+++ b/solution.py
@@ -213,7 +213,7 @@
     tall = lhs.shape[0] // 4
     wide = expand_ref.shape[2]
     shifts = sorted(range(1, parts), key=lambda s: (abs(2 * s - parts), s))
-    fields = (0, 2, 1)
+    fields = (2, 0, 1)
 
     loads = {}
 
@@ -224,13 +224,19 @@
     def slab_of(shift):
         return lax.rem(me + shift, parts)
 
-    load(("x", 0), x_hbm.at[0], x_ref.at[0])
-    for shift in shifts + [0]:
-        load(("reduce", shift), reduce_hbm.at[slab_of(shift)], reduce_ref.at[shift])
-    load(("x", 2), x_hbm.at[2], x_ref.at[2])
-    load(("x", 1), x_hbm.at[1], x_ref.at[1])
-    load("table", table_hbm, table_ref)
-    load("expand", expand_hbm, expand_ref)
+    def rest():
+        for shift in shifts[1:] + [0]:
+            load(("reduce", shift), reduce_hbm.at[slab_of(shift)], reduce_ref.at[shift])
+        for f in fields[1:]:
+            load(("x", f), x_hbm.at[f], x_ref.at[f])
+        load("table", table_hbm, table_ref)
+        load("expand", expand_hbm, expand_ref)
+
+    first = fields[0]
+    load(("x", first, 0), x_hbm.at[first, 0], x_ref.at[first, 0])
+    load(("reduce", shifts[0]), reduce_hbm.at[slab_of(shifts[0])], reduce_ref.at[shifts[0]])
+    for j in range(1, planes):
+        load(("x", first, j), x_hbm.at[first, j], x_ref.at[first, j])
 
     @pl.when(level == 0)
     def _():
@@ -241,15 +247,13 @@
         halo[:, 1] = jnp.zeros_like(halo[:, 1])
 
     barrier = pltpu.get_barrier_semaphore()
-    for shift in range(1, parts):
-        pl.semaphore_signal(
-            barrier, inc=1, device_id={"pa": slab_of(shift)}, device_id_type=MESH
-        )
-    for shift in range(1, levels):
-        pl.semaphore_signal(
-            barrier, inc=1, device_id={"gy": lax.rem(level + shift, levels)}, device_id_type=MESH
-        )
-    pl.semaphore_wait(barrier, parts + levels - 2)
+    others = [(a, b) for a in range(levels) for b in range(parts) if a or b]
+
+    def other(a, b):
+        return {"gy": lax.rem(level + a, levels), "pa": lax.rem(me + b, parts)}
+
+    for a, b in others:
+        pl.semaphore_signal(barrier, inc=1, device_id=other(a, b), device_id_type=MESH)
 
     def transfer(f, j, shift):
         return pltpu.make_async_remote_copy(
@@ -264,90 +268,112 @@
     def arrive(f, j):
         for shift in shifts:
             transfer(f, j, shift).wait_recv()
-
-    def reduce_field(f):
-        loads["x", f].wait()
+            if f in (0, 2):
+                halo_start(f, j, shift)
+
+    def turn_modes(f, j):
+        lanes = slice(j * kx_local, (j + 1) * kx_local)
 
         @pl.loop(0, width // 128)
         def _(n):
             at = pl.ds(pl.multiple_of(n * 128, 128), 128)
+            tile[j] = x_ref[f, j, :, at]
+            rows = jnp.concatenate((
+                tile[j, pl.ds(0, kx_local // 2, stride=2), :],
+                tile[j, pl.ds(1, kx_local // 2, stride=2), :],
+            ))
+            high, low = split(rows.T)
+            xt_ref[0, at, lanes] = high
+            xt_ref[1, at, lanes] = low
+
+    def reduce_slab(f, shift, which):
+        lanes = slice(which[0] * kx_local, (which[-1] + 1) * kx_local)
+        both = dot(reduce_ref[shift], xt_ref[0, :, lanes])
+        out = both[:two] + both[two:] + dot(reduce_ref[shift, :two, :], xt_ref[1, :, lanes])
+        for n, j in enumerate(which):
+            real = out[:rank, n * kx_local : (n + 1) * kx_local]
+            imag = out[rank:, n * kx_local : (n + 1) * kx_local]
+            left = lax.broadcasted_iota(jnp.int32, real.shape, 1) < kx_local // 2
+            even = jnp.where(left, real, pltpu.roll(imag, kx_local // 2, 1))
+            odd = jnp.where(left, pltpu.roll(real, kx_local // 2, 1), imag)
+            if shift:
+                send[f, j, shift - 1, half(0), :] = even
+                send[f, j, shift - 1, half(1), :] = odd
+            else:
+                recv[f, j, me, half(0), :] = even
+                recv[f, j, me, half(1), :] = odd
+
+    def reduce_first(f):
+        for j in range(planes):
+            loads["x", f, j].wait()
+            if j == planes - 1:
+                rest()
+            turn_modes(f, j)
+            if j == 0:
+                loads["reduce", shifts[0]].wait()
+            reduce_slab(f, shifts[0], (j,))
+            if j == 0:
+                pl.semaphore_wait(barrier, len(others))
+            transfer(f, j, shifts[0]).start()
+        for shift in shifts[1:] + [0]:
+            loads["reduce", shift].wait()
+            reduce_slab(f, shift, range(planes))
             for j in range(planes):
-                tile[j] = x_ref[f, j, :, at]
-                rows = jnp.concatenate((
-                    tile[j, pl.ds(0, kx_local // 2, stride=2), :],
-                    tile[j, pl.ds(1, kx_local // 2, stride=2), :],
-                ))
-                high, low = split(rows.T)
-                lanes = slice(j * kx_local, (j + 1) * kx_local)
-                xt_ref[0, at, lanes] = high
-                xt_ref[1, at, lanes] = low
-
+                if shift:
+                    transfer(f, j, shift).start()
+                else:
+                    halo_start(f, j, 0)
+
+    def reduce_field(f):
+        loads["x", f].wait()
+        for j in range(planes):
+            turn_modes(f, j)
         for shift in shifts + [0]:
-            if f == fields[0]:
-                loads["reduce", shift].wait()
-            both = dot(reduce_ref[shift], xt_ref[0])
-            out = both[:two] + both[two:] + dot(reduce_ref[shift, :two, :], xt_ref[1])
+            reduce_slab(f, shift, range(planes))
+        if f == 0:
             for j in range(planes):
-                real = out[:rank, j * kx_local : (j + 1) * kx_local]
-                imag = out[rank:, j * kx_local : (j + 1) * kx_local]
-                first = lax.broadcasted_iota(jnp.int32, real.shape, 1) < kx_local // 2
-                even = jnp.where(first, real, pltpu.roll(imag, kx_local // 2, 1))
-                odd = jnp.where(first, pltpu.roll(real, kx_local // 2, 1), imag)
-                if shift:
-                    send[f, j, shift - 1, half(0), :] = even
-                    send[f, j, shift - 1, half(1), :] = odd
-                else:
-                    recv[f, j, me, half(0), :] = even
-                    recv[f, j, me, half(1), :] = odd
-            if shift and f == fields[0]:
-                for j in range(planes):
-                    transfer(f, j, shift).start()
-
-    def follow(f, before):
-        for j in range(planes):
-            for shift in shifts:
-                transfer(before, j, shift).wait_send()
-                transfer(f, j, shift).start()
-
-    def halo_copy(f, up):
-        if up:
-            return pltpu.make_async_remote_copy(
-                src_ref=recv.at[f, planes - 1], dst_ref=halo.at[f // 2, 0],
-                send_sem=halo_send.at[f // 2, 0], recv_sem=halo_recv.at[f // 2, 0],
-                device_id={"gy": lax.rem(level + 1, levels)}, device_id_type=MESH,
-            )
+                halo_start(f, j, 0)
+
+    def follow(f, j, before, k):
+        for shift in shifts:
+            transfer(before, k, shift).wait_send()
+            transfer(f, j, shift).start()
+
+    def halo_copy(f, up, shift):
+        source = lax.rem(me + parts - shift, parts)
+        side, j, step = (0, planes - 1, 1) if up else (1, 0, levels - 1)
         return pltpu.make_async_remote_copy(
-            src_ref=recv.at[f, 0], dst_ref=halo.at[f // 2, 1],
-            send_sem=halo_send.at[f // 2, 1], recv_sem=halo_recv.at[f // 2, 1],
-            device_id={"gy": lax.rem(level + levels - 1, levels)}, device_id_type=MESH,
+            src_ref=recv.at[f, j, source], dst_ref=halo.at[f // 2, side, source],
+            send_sem=halo_send.at[f // 2, side, shift], recv_sem=halo_recv.at[f // 2, side, shift],
+            device_id={"gy": lax.rem(level + step, levels)}, device_id_type=MESH,
         )
 
-    def halo_start(f):
-        @pl.when(level < levels - 1)
+    def halo_start(f, j, shift):
+        @pl.when(level < levels - 1 if j else level > 0)
         def _():
-            halo_copy(f, True).start()
-
-        @pl.when(level > 0)
-        def _():
-            halo_copy(f, False).start()
+            halo_copy(f, j > 0, shift).start()
 
     def halo_arrive(f):
         @pl.when(level > 0)
         def _():
-            halo_copy(f, True).wait_recv()
+            for shift in range(parts):
+                halo_copy(f, True, shift).wait_recv()
 
         @pl.when(level < levels - 1)
         def _():
-            halo_copy(f, False).wait_recv()
+            for shift in range(parts):
+                halo_copy(f, False, shift).wait_recv()
 
     def halo_sent(f):
         @pl.when(level < levels - 1)
         def _():
-            halo_copy(f, True).wait_send()
+            for shift in range(parts):
+                halo_copy(f, True, shift).wait_send()
 
         @pl.when(level > 0)
         def _():
-            halo_copy(f, False).wait_send()
+            for shift in range(parts):
+                halo_copy(f, False, shift).wait_send()
 
     def fill(slot, hat):
         @pl.loop(0, parts)
@@ -414,32 +440,16 @@
             return step(at, ((slice(0, TILE), at), (slice(TILE, 2 * TILE), far)), carry)
         return lax.fori_loop(0, NX // 2 // TILE, at_tile, init)
 
-    for f in fields:
+    reduce_first(first)
+    for f in fields[1:]:
         reduce_field(f)
     loads["table"].wait()
     loads["expand"].wait()
 
-    follow(2, 0)
     for j in range(planes):
-        arrive(0, j)
-    halo_start(0)
-    for j in range(planes):
-        fill(j, modes(0, j))
-
-    def u_tile(at, sides, carry):
-        for j, value in enumerate(to_x(at)):
-            both = to_z(value, 2 * slab)
-            for part, to in sides:
-                lamb_ref[0, j, :, to] = both[:slab, part]
-                lamb_ref[2, j, :, to] = both[slab:, part]
-        return carry
-
-    tiles(u_tile, 0)
-
-    follow(1, 2)
+        follow(0, j, 2, j)
     for j in range(planes):
         arrive(2, j)
-    halo_start(2)
     for j in range(planes):
         fill(0, modes(2, j))
         fill(1, turned(2, j))
@@ -449,12 +459,12 @@
             w, dx_w = to_z(w, slab), to_z(dx_w, slab)
             for part, to in sides:
                 lamb_ref[1, j, :, to] = w[:, part]
-                lamb_ref[2, j, :, to] = lamb_ref[2, j, :, to] - dx_w[:, part]
+                lamb_ref[2, j, :, to] = dx_w[:, part]
             return carry
 
         tiles(w_tile, 0)
 
-    halo_arrive(0)
+    arrive(0, 0)
     halo_arrive(2)
     for j in range(planes):
         fill(j, slope_y(2, j))
@@ -467,6 +477,25 @@
         return carry
 
     tiles(dy_tile, 0)
+
+    follow(1, 0, 0, 1)
+    for shift in shifts:
+        transfer(0, 0, shift).wait_send()
+        transfer(1, 1, shift).start()
+    arrive(0, 1)
+    for j in range(planes):
+        fill(j, modes(0, j))
+
+    def u_tile(at, sides, carry):
+        for j, value in enumerate(to_x(at)):
+            both = to_z(value, 2 * slab)
+            for part, to in sides:
+                lamb_ref[0, j, :, to] = both[:slab, part]
+                lamb_ref[2, j, :, to] = both[slab:, part] - lamb_ref[2, j, :, to]
+        return carry
+
+    tiles(u_tile, 0)
+    halo_arrive(0)
 
     top = jnp.zeros((8, TILE), jnp.float32)
     for j in range(planes):
@@ -491,27 +520,23 @@
 
         top = tiles(v_tile, top)
 
-    def peak_copy(axis, count, base, here, shift):
-        return pltpu.make_async_remote_copy(
-            src_ref=peaks.at[base], dst_ref=peaks.at[base + shift],
-            send_sem=peak_send.at[base + shift], recv_sem=peak_recv.at[base + shift],
-            device_id={axis: lax.rem(here + shift, count)}, device_id_type=MESH,
-        )
-
     value = top[:, :128]
     for k in range(1, TILE // 128):
         value = jnp.maximum(value, top[:, k * 128 : (k + 1) * 128])
-    base = 0
-    for axis, count, here in (("gy", levels, level), ("pa", parts, me)):
-        peaks[base] = value
-        copies = [peak_copy(axis, count, base, here, shift) for shift in range(1, count)]
-        for copy in copies:
-            copy.start()
-        for copy in copies:
-            copy.wait()
-        for shift in range(1, count):
-            value = jnp.maximum(value, peaks[base + shift])
-        base += count
+    peaks[0] = value
+    copies = [
+        pltpu.make_async_remote_copy(
+            src_ref=peaks.at[0], dst_ref=peaks.at[n + 1],
+            send_sem=peak_send.at[n], recv_sem=peak_recv.at[n],
+            device_id=other(a, b), device_id_type=MESH,
+        )
+        for n, (a, b) in enumerate(others)
+    ]
+    for copy in copies:
+        copy.start()
+    for copy in copies:
+        copy.wait_recv()
+    value = peaks[...].max(0)
     peak = jnp.sqrt(jnp.max(value, axis=(0, 1), keepdims=True))
     scale = 1.0 / (peak + 1e-06)
 
@@ -522,13 +547,15 @@
             for j in range(planes):
                 lamb_ref[c, j, rows, :] = lamb_ref[c, j, rows, :] * scale
 
-    peak_ref[...] = jnp.broadcast_to(peak, peak_ref.shape)
+    peak_ref[...] = peak
 
     for j in range(planes):
         for shift in shifts:
             transfer(1, j, shift).wait_send()
     halo_sent(0)
     halo_sent(2)
+    for copy in copies:
+        copy.wait_send()
 
 
 def body(spectral_velocity, inverse_spacing):
@@ -548,7 +575,7 @@
         functools.partial(field_kernel, parts, levels, rank),
         out_shape=(
             pltpu.VMEM((3, planes, slab, NX), jnp.float32),
-            jax.ShapeDtypeStruct((8, 128), jnp.float32),
+            jax.ShapeDtypeStruct((1, 1), jnp.float32),
         ),
         in_specs=[vmem, pl.BlockSpec(memory_space=pltpu.SMEM), hbm, hbm, hbm, hbm],
         out_specs=(vmem, vmem),
@@ -563,15 +590,15 @@
             pltpu.VMEM((2, 2) + block, jnp.float32),
             pltpu.VMEM((4 * tall, 2 * KX), jnp.bfloat16),
             pltpu.VMEM((planes, slab, NX), jnp.float32),
-            pltpu.VMEM((parts + levels, 8, 128), jnp.float32),
+            pltpu.VMEM((parts * levels, 8, 128), jnp.float32),
             pltpu.VMEM((planes, kx_local, 128), jnp.float32),
-            dma((parts + 5,)),
+            dma((parts + 6,)),
             dma((3, planes, parts)),
             dma((3, planes, parts)),
-            dma((2, 2)),
-            dma((2, 2)),
-            dma((parts + levels,)),
-            dma((parts + levels,)),
+            dma((2, 2, parts)),
+            dma((2, 2, parts)),
+            dma((parts * levels - 1,)),
+            dma((parts * levels - 1,)),
         ],
         compiler_params=pltpu.CompilerParams(
             collective_id=0, has_side_effects=True, vmem_limit_bytes=51 * 2**20

time: 159 us -> 144 us (0.906)
  Pallas kernels: 153 us -> 137 us
  between operations: 0.64 us -> 2.33 us
    pallas_call x1, Pallas kernels: 153 us -> 137 us  [body(): pl.pallas_call(functools.partial(field_kernel, parts, levels, rank), out_...]
where the time goes in v3:
time: 144 us
  Pallas kernels  137 us (95%)
  local copies, waits for them, and re-layouts  4.13 us (3%)
  between operations  2.33 us (2%)
    pallas_call x1, Pallas kernels, body(): pl.pallas_call(functools.partial(field_kernel, parts, levels, rank), out_...  137 us
    unnamed x1, local copies, waits for them, and re-layouts  4.13 us

profile of v3, /device:TPU:0, one launch (start us, length us, event | category | flops | bytes accessed | tf_op | source)
XLA Modules:
  0.0 143.8 jit_solution(4736812363089382738)
XLA Ops:
  0.6 137.3 %shard_map.77 = (f32[3,2,288,1536]{3,2,1,0:T(8,128)S(1)}, f32[1,1]{1,0:T(1,128)}) custom-call(f32[2,8,512]{2,1,0:T(8,128)} %constant.8.clone.wave_ref, f32[2]{0:T(128)} %space_ref.1, f32[3,2,128,1536]{3,2,1,0:T(8,128)} %x_hbm.1, bf16[4,864,1536]{2,1,0:T(8,128)(2,1)} %constant.9.clone.reduce_hbm, bf16[2,576,256]{2,1,0:T(8,128)(2,1)} %constant.10.clone.expand_hbm, ...), custom_call_target="tpu_custom_call" | custom-call | tf_op jit(solution)/shard_map/pallas_call | solution.py:574
  138.0 4.1 %copy.10 = f32[3,2,288,1536]{3,2,1,0:T(8,128)} copy(f32[3,2,288,1536]{3,2,1,0:T(8,128)S(1)} %get-tuple-element.6) | data formatting | bytes 21233664

commit v4 on v3

--- a/solution.py
+++ b/solution.py
@@ -203,7 +203,7 @@
 def field_kernel(
     parts, levels, rank, wave_ref, space_ref, x_hbm, reduce_hbm, expand_hbm, table_hbm,
     lamb_ref, peak_ref,
-    x_ref, xt_ref, reduce_ref, expand_ref, table_ref, send, recv, halo, lhs, part_x, peaks, tile,
+    x_ref, xt_ref, reduce_ref, expand_ref, table_ref, send, recv, halo, lhs, part_x, peaks, tile, even_ref,
     load_sem, send_sem, recv_sem, halo_send, halo_recv, peak_send, peak_recv,
 ):
     me, level = lax.axis_index("pa"), lax.axis_index("gy")
@@ -255,12 +255,17 @@
     for a, b in others:
         pl.semaphore_signal(barrier, inc=1, device_id=other(a, b), device_id_type=MESH)
 
-    def transfer(f, j, shift):
+    def half(c):
+        return slice(c * rank, (c + 1) * rank)
+
+    def transfer(f, j, shift, c=None):
+        rows = slice(0, two) if c is None else half(c)
+        at = j + (c or 0)
         return pltpu.make_async_remote_copy(
-            src_ref=send.at[f, j, shift - 1],
-            dst_ref=recv.at[f, j, me],
-            send_sem=send_sem.at[f, j, shift],
-            recv_sem=recv_sem.at[f, j, shift],
+            src_ref=send.at[f, j, shift - 1, rows],
+            dst_ref=recv.at[f, j, me, rows],
+            send_sem=send_sem.at[f, at, shift],
+            recv_sem=recv_sem.at[f, at, shift],
             device_id={"pa": slab_of(shift)},
             device_id_type=MESH,
         )
@@ -375,11 +380,11 @@
             for shift in range(parts):
                 halo_copy(f, False, shift).wait_send()
 
-    def fill(slot, hat):
+    def fill(slot, hat, classes=(0, 1)):
         @pl.loop(0, parts)
         def _(source):
             here = pl.multiple_of(source * kx_local, kx_local)
-            for c in range(2):
+            for c in classes:
                 value = hat(source, here, c)
                 if tall > rank:
                     value = jnp.concatenate((value, jnp.zeros((tall - rank, kx_local), jnp.float32)))
@@ -387,9 +392,6 @@
                 lanes = pl.ds(pl.multiple_of(c * KX + here, kx_local), kx_local)
                 lhs[slot * tall : (slot + 1) * tall, lanes] = high
                 lhs[(2 + slot) * tall : (3 + slot) * tall, lanes] = low
-
-    def half(c):
-        return slice(c * rank, (c + 1) * rank)
 
     def modes(f, j):
         return lambda source, here, c: recv[f, j, source, half(c), :]
@@ -413,13 +415,14 @@
     def minus(first, second):
         return lambda source, here, c: first(source, here, c) - second(source, here, c)
 
-    def to_x(at):
-        def of(c):
-            lanes = slice(c * KX, (c + 1) * KX)
-            both = dot(lhs[:, lanes], table_ref[0, c, :, at])
-            return both[: 2 * tall] + both[2 * tall :] + dot(lhs[: 2 * tall, lanes], table_ref[1, c, :, at])
-
-        even, odd = of(0), of(1)
+    def of_class(c, at):
+        lanes = slice(c * KX, (c + 1) * KX)
+        both = dot(lhs[:, lanes], table_ref[0, c, :, at])
+        return both[: 2 * tall] + both[2 * tall :] + dot(lhs[: 2 * tall, lanes], table_ref[1, c, :, at])
+
+    def to_x(at, even=None):
+        even = of_class(0, at) if even is None else even
+        odd = of_class(1, at)
         out = jnp.concatenate((even + odd, even - odd), 1)
         return out[:tall], out[tall:]
 
@@ -433,12 +436,12 @@
             + dot(expand_ref[0, :rows, :], low)
         )
 
-    def tiles(step, init):
+    def tiles(step, init, unroll=False):
         def at_tile(t, carry):
             at = pl.ds(pl.multiple_of(t * TILE, TILE), TILE)
             far = pl.ds(pl.multiple_of(NX // 2 + t * TILE, TILE), TILE)
             return step(at, ((slice(0, TILE), at), (slice(TILE, 2 * TILE), far)), carry)
-        return lax.fori_loop(0, NX // 2 // TILE, at_tile, init)
+        return lax.fori_loop(0, NX // 2 // TILE, at_tile, init, unroll=unroll)
 
     reduce_first(first)
     for f in fields[1:]:
@@ -479,9 +482,12 @@
     tiles(dy_tile, 0)
 
     follow(1, 0, 0, 1)
+    last = planes - 1
     for shift in shifts:
         transfer(0, 0, shift).wait_send()
-        transfer(1, 1, shift).start()
+        transfer(1, last, shift, 0).start()
+    for shift in shifts:
+        transfer(1, last, shift, 1).start()
     arrive(0, 1)
     for j in range(planes):
         fill(j, modes(0, j))
@@ -499,12 +505,26 @@
 
     top = jnp.zeros((8, TILE), jnp.float32)
     for j in range(planes):
-        arrive(1, j)
-        fill(0, modes(1, j))
-        fill(1, minus(turned(1, j), slope_y(0, j)))
+        hats = modes(1, j), minus(turned(1, j), slope_y(0, j))
+        if j < last:
+            arrive(1, j)
+            for slot in range(2):
+                fill(slot, hats[slot])
+        else:
+            for c in range(2):
+                for shift in shifts:
+                    transfer(1, last, shift, c).wait_recv()
+                for slot in range(2):
+                    fill(slot, hats[slot], (c,))
+                if c == 0:
+                    def even_tile(at, sides, carry):
+                        even_ref[:, at] = of_class(0, at)
+                        return carry
+
+                    tiles(even_tile, 0)
 
         def v_tile(at, sides, top):
-            value, turn = to_x(at)
+            value, turn = to_x(at, even_ref[:, at] if j == last else None)
             value = to_z(value, 2 * slab)
             turn = to_z(turn, slab)
             for part, to in sides:
@@ -518,12 +538,12 @@
                 top = jnp.maximum(top, square.reshape(slab // 8, 8, TILE).max(0))
             return top
 
-        top = tiles(v_tile, top)
+        top = tiles(v_tile, top, j == last)
 
     value = top[:, :128]
     for k in range(1, TILE // 128):
         value = jnp.maximum(value, top[:, k * 128 : (k + 1) * 128])
-    peaks[0] = value
+    peaks[0] = value.max(0, keepdims=True)
     copies = [
         pltpu.make_async_remote_copy(
             src_ref=peaks.at[0], dst_ref=peaks.at[n + 1],
@@ -538,24 +558,44 @@
         copy.wait_recv()
     value = peaks[...].max(0)
     peak = jnp.sqrt(jnp.max(value, axis=(0, 1), keepdims=True))
-    scale = 1.0 / (peak + 1e-06)
-
-    @pl.loop(0, slab // 16)
-    def _(n):
-        rows = pl.ds(pl.multiple_of(n * 16, 16), 16)
-        for c in range(3):
-            for j in range(planes):
-                lamb_ref[c, j, rows, :] = lamb_ref[c, j, rows, :] * scale
-
-    peak_ref[...] = peak
-
-    for j in range(planes):
-        for shift in shifts:
+    peak_ref[...] = jnp.broadcast_to(peak, peak_ref.shape)
+
+    for shift in shifts:
+        for j in range(last):
             transfer(1, j, shift).wait_send()
+        for c in range(2):
+            transfer(1, last, shift, c).wait_send()
     halo_sent(0)
     halo_sent(2)
     for copy in copies:
         copy.wait_send()
+
+
+def scale_kernel(lamb_ref, peak_ref, out_hbm, top_ref, held, sem):
+    top_ref[...] = peak_ref[0:1, 0:1]
+    scale = 1.0 / (peak_ref[0:1, 0:1] + 1e-06)
+    slots, rows, _ = held.shape
+    per = lamb_ref.shape[2] // rows
+    places = [
+        (c, j, k) for c in range(lamb_ref.shape[0]) for j in range(lamb_ref.shape[1]) for k in range(per)
+    ]
+    copies = []
+    for n, (c, j, k) in enumerate(places):
+        at = pl.ds(k * rows, rows)
+        if n >= slots:
+            copies[n - slots].wait()
+
+        @pl.loop(0, rows // 16)
+        def _(i):
+            part = pl.ds(pl.multiple_of(i * 16, 16), 16)
+            held[n % slots, part, :] = lamb_ref[c, j, pl.ds(pl.multiple_of(k * rows + i * 16, 16), 16), :] * scale
+
+        copies.append(pltpu.make_async_copy(
+            held.at[n % slots], out_hbm.at[c, j, at], sem.at[n % slots]
+        ))
+        copies[n].start()
+    for copy in copies[-slots:]:
+        copy.wait()
 
 
 def body(spectral_velocity, inverse_spacing):
@@ -575,7 +615,7 @@
         functools.partial(field_kernel, parts, levels, rank),
         out_shape=(
             pltpu.VMEM((3, planes, slab, NX), jnp.float32),
-            jax.ShapeDtypeStruct((1, 1), jnp.float32),
+            pltpu.VMEM((8, 128), jnp.float32),
         ),
         in_specs=[vmem, pl.BlockSpec(memory_space=pltpu.SMEM), hbm, hbm, hbm, hbm],
         out_specs=(vmem, vmem),
@@ -590,11 +630,12 @@
             pltpu.VMEM((2, 2) + block, jnp.float32),
             pltpu.VMEM((4 * tall, 2 * KX), jnp.bfloat16),
             pltpu.VMEM((planes, slab, NX), jnp.float32),
-            pltpu.VMEM((parts * levels, 8, 128), jnp.float32),
+            pltpu.VMEM((parts * levels, 1, 128), jnp.float32),
             pltpu.VMEM((planes, kx_local, 128), jnp.float32),
+            pltpu.VMEM((2 * tall, NX // 2), jnp.float32),
             dma((parts + 6,)),
-            dma((3, planes, parts)),
-            dma((3, planes, parts)),
+            dma((3, planes + 1, parts)),
+            dma((3, planes + 1, parts)),
             dma((2, 2, parts)),
             dma((2, 2, parts)),
             dma((parts * levels - 1,)),
@@ -604,7 +645,21 @@
             collective_id=0, has_side_effects=True, vmem_limit_bytes=51 * 2**20
         ),
     )(wave, inverse_spacing, spectral_velocity, reduce, expand, table)
-    return lamb, peak[0, 0]
+    out, top = pl.pallas_call(
+        scale_kernel,
+        out_shape=(
+            jax.ShapeDtypeStruct(lamb.shape, jnp.float32),
+            jax.ShapeDtypeStruct((1, 1), jnp.float32),
+        ),
+        in_specs=[vmem, vmem],
+        out_specs=(hbm, vmem),
+        scratch_shapes=[pltpu.VMEM((8, slab // 6, NX), jnp.float32), dma((8,))],
+        compiler_params=pltpu.CompilerParams(vmem_limit_bytes=6 * 2**20),
+    )(
+        pltpu.with_memory_space_constraint(lamb, pltpu.VMEM),
+        pltpu.with_memory_space_constraint(peak, pltpu.VMEM),
+    )
+    return out, top[0, 0]
 
 
 def solution(mesh):

time: 144 us -> 141 us (0.979)
  local copies, waits for them, and re-layouts: 4.13 us -> 0 us
  Pallas kernels: 137 us -> 140 us
  between operations: 2.33 us -> 0.8 us
    pallas_call x0 -> x1, Pallas kernels: none -> 4.7 us  [body(): pl.pallas_call(scale_kernel, out_shape=(jax.ShapeDtypeStruct(lamb.shape,...]
    unnamed x1 -> x0, local copies, waits for them, and re-layouts: 4.13 us -> none
    pallas_call x1, Pallas kernels: 137 us -> 135 us  [body(): pl.pallas_call(functools.partial(field_kernel, parts, levels, rank), out_...]
where the time goes in v4:
time: 141 us
  Pallas kernels  140 us (99%)
    pallas_call x1, Pallas kernels, body(): pl.pallas_call(functools.partial(field_kernel, parts, levels, rank), out_...  135 us
    pallas_call x1, Pallas kernels, body(): pl.pallas_call(scale_kernel, out_shape=(jax.ShapeDtypeStruct(lamb.shape,...  4.7 us

profile of v4, /device:TPU:0, one launch (start us, length us, event | category | flops | bytes accessed | tf_op | source)
XLA Modules:
  0.0 140.7 jit_solution(4288820856061902264)
XLA Ops:
  0.6 135.2 %shard_map.77 = (f32[3,2,288,1536]{3,2,1,0:T(8,128)S(1)}, f32[8,128]{1,0:T(8,128)S(1)}) custom-call(f32[2,8,512]{2,1,0:T(8,128)} %constant.8.clone.wave_ref, f32[2]{0:T(128)} %space_ref.1, f32[3,2,128,1536]{3,2,1,0:T(8,128)} %x_hbm.1, bf16[4,864,1536]{2,1,0:T(8,128)(2,1)} %constant.9.clone.reduce_hbm, bf16[2,576,256]{2,1,0:T(8,128)(2,1)} %constant.10.clone.expand_hbm, ...), custom_call_target="tpu_custom_call" | custom-call | tf_op jit(solution)/shard_map/pallas_call | solution.py:614
  135.8 4.7 %shard_map.78 = (f32[3,2,288,1536]{3,2,1,0:T(8,128)}, f32[1,1]{1,0:T(1,128)}) custom-call(f32[3,2,288,1536]{3,2,1,0:T(8,128)S(1)} %get-tuple-element.6.lamb_ref, f32[8,128]{1,0:T(8,128)S(1)} %get-tuple-element.7.peak_ref), custom_call_target="tpu_custom_call" | custom-call | tf_op jit(solution)/shard_map/pallas_call | solution.py:648

commit v5 on v4

--- a/solution.py
+++ b/solution.py
@@ -201,9 +201,9 @@
 
 
 def field_kernel(
-    parts, levels, rank, wave_ref, space_ref, x_hbm, reduce_hbm, expand_hbm, table_hbm,
+    parts, levels, rank, wave_hbm, space_ref, x_hbm, reduce_hbm, expand_hbm, table_hbm,
     lamb_ref, peak_ref,
-    x_ref, xt_ref, reduce_ref, expand_ref, table_ref, send, recv, halo, lhs, part_x, peaks, tile, even_ref,
+    x_ref, xt_ref, reduce_ref, expand_ref, table_ref, send, recv, halo, lhs, part_x, peaks, tile, even_ref, wave_ref,
     load_sem, send_sem, recv_sem, halo_send, halo_recv, peak_send, peak_recv,
 ):
     me, level = lax.axis_index("pa"), lax.axis_index("gy")
@@ -231,6 +231,7 @@
             load(("x", f), x_hbm.at[f], x_ref.at[f])
         load("table", table_hbm, table_ref)
         load("expand", expand_hbm, expand_ref)
+        load("wave", wave_hbm, wave_ref)
 
     first = fields[0]
     load(("x", first, 0), x_hbm.at[first, 0], x_ref.at[first, 0])
@@ -279,13 +280,12 @@
     def turn_modes(f, j):
         lanes = slice(j * kx_local, (j + 1) * kx_local)
 
-        @pl.loop(0, width // 128)
-        def _(n):
-            at = pl.ds(pl.multiple_of(n * 128, 128), 128)
-            tile[j] = x_ref[f, j, :, at]
+        for n in range(width // 128):
+            at = slice(n * 128, (n + 1) * 128)
+            tile[n] = x_ref[f, j, :, at]
             rows = jnp.concatenate((
-                tile[j, pl.ds(0, kx_local // 2, stride=2), :],
-                tile[j, pl.ds(1, kx_local // 2, stride=2), :],
+                tile[n, pl.ds(0, kx_local // 2, stride=2), :],
+                tile[n, pl.ds(1, kx_local // 2, stride=2), :],
             ))
             high, low = split(rows.T)
             xt_ref[0, at, lanes] = high
@@ -448,6 +448,7 @@
         reduce_field(f)
     loads["table"].wait()
     loads["expand"].wait()
+    loads["wave"].wait()
 
     for j in range(planes):
         follow(0, j, 2, j)
@@ -617,7 +618,7 @@
             pltpu.VMEM((3, planes, slab, NX), jnp.float32),
             pltpu.VMEM((8, 128), jnp.float32),
         ),
-        in_specs=[vmem, pl.BlockSpec(memory_space=pltpu.SMEM), hbm, hbm, hbm, hbm],
+        in_specs=[hbm, pl.BlockSpec(memory_space=pltpu.SMEM), hbm, hbm, hbm, hbm],
         out_specs=(vmem, vmem),
         scratch_shapes=[
             pltpu.VMEM((3, planes, kx_local, width), jnp.float32),
@@ -631,9 +632,10 @@
             pltpu.VMEM((4 * tall, 2 * KX), jnp.bfloat16),
             pltpu.VMEM((planes, slab, NX), jnp.float32),
             pltpu.VMEM((parts * levels, 1, 128), jnp.float32),
-            pltpu.VMEM((planes, kx_local, 128), jnp.float32),
+            pltpu.VMEM((width // 128, kx_local, 128), jnp.float32),
             pltpu.VMEM((2 * tall, NX // 2), jnp.float32),
-            dma((parts + 6,)),
+            pltpu.VMEM(wave.shape, jnp.float32),
+            dma((parts + 7,)),
             dma((3, planes + 1, parts)),
             dma((3, planes + 1, parts)),
             dma((2, 2, parts)),

time: 141 us -> 140 us (level)
  no operation moved by 1% of the time
where the time goes in v5:
time: 140 us
  Pallas kernels  139 us (99%)
    pallas_call x1, Pallas kernels, body(): pl.pallas_call(functools.partial(field_kernel, parts, levels, rank), out_...  135 us
    pallas_call x1, Pallas kernels, body(): pl.pallas_call(scale_kernel, out_shape=(jax.ShapeDtypeStruct(lamb.shape,...  4.7 us

profile of v5, /device:TPU:0, one launch (start us, length us, event | category | flops | bytes accessed | tf_op | source)
XLA Modules:
  0.0 140.0 jit_solution(18315963152204490242)
XLA Ops:
  0.6 134.5 %shard_map.77 = (f32[3,2,288,1536]{3,2,1,0:T(8,128)S(1)}, f32[8,128]{1,0:T(8,128)S(1)}) custom-call(f32[2,8,512]{2,1,0:T(8,128)} %constant.8.clone.wave_hbm, f32[2]{0:T(128)} %space_ref.1, f32[3,2,128,1536]{3,2,1,0:T(8,128)} %x_hbm.1, bf16[4,864,1536]{2,1,0:T(8,128)(2,1)} %constant.9.clone.reduce_hbm, bf16[2,576,256]{2,1,0:T(8,128)(2,1)} %constant.10.clone.expand_hbm, ...), custom_call_target="tpu_custom_call" | custom-call | tf_op jit(solution)/shard_map/pallas_call | solution.py:615
  135.2 4.7 %shard_map.78 = (f32[3,2,288,1536]{3,2,1,0:T(8,128)}, f32[1,1]{1,0:T(1,128)}) custom-call(f32[3,2,288,1536]{3,2,1,0:T(8,128)S(1)} %get-tuple-element.6.lamb_ref, f32[8,128]{1,0:T(8,128)S(1)} %get-tuple-element.7.peak_ref), custom_call_target="tpu_custom_call" | custom-call | tf_op jit(solution)/shard_map/pallas_call | solution.py:650
